TPU v7x, 128 devices: a whole 4x4x4 slice. The times are simulated.
128 devices in a mesh: cluster: 16 (over y, z), blk: 8 (over x, core).
Axes of the slice: x: 4, y: 4, z: 4, core: 2. Of those that a mesh axis runs over, the one named last changes fastest.
Arguments:
- rhs_block: float32 [2, 32, 16384], P(None, None, ('cluster', 'blk')), may hold values from -6 to 6
- far_row_factor: bfloat16 [8192, 2, 128, 128], P(('cluster', 'blk')), may hold values from -0.5 to 0.5
- far_col_factor: bfloat16 [8192, 2, 128, 128], P(('cluster', 'blk')), may hold values from -0.0625 to 0.0625
- far_rank: int32 [8192], P(('cluster', 'blk')), may hold values from 8 to 128
- far_row_leaf: int32 [8192], P(('cluster', 'blk')), may hold values from 0 to 127, as said below
- far_block_column_leaf: int32 [8192], P(('cluster', 'blk')), may hold values from 0 to 127, as said below
- near_matrix: bfloat16 [4096, 2, 128, 128], P(('cluster', 'blk'))
- near_col_leaf: int32 [4096], P(('cluster', 'blk')), may hold values from 0 to 127, as said below
- near_offset: int32 [4096], P(('cluster', 'blk')), may hold values from -2 to 2
Outputs:
- krylov_last: float32 [2, 32, 16384], P(None, None, ('cluster', 'blk'))
- hessenberg: float32 [32, 8], replicated
Inputs may be any that keep to these rules, and one draw needn't show every extreme that they name: far block k lies in the column cluster of its devices: far_block_column_leaf[k] // 8 equals k // (64 times the size of blk). near block k lies in the column cluster of its devices: near_col_leaf[k] // 8 equals k // (32 times the size of blk). `far_row_leaf`: the far blocks of one device (aligned runs of 64 blocks) read exactly 4 distinct row leaves of every segment of 8 leaves.
All inputs are finite; a program needn't handle non-finite values.
Results may differ from a plain program's by a relative error of at most 0.0072.
Values may be sent and summed in bfloat16 or wider, within the bound.
A program may use at most 64 MiB of HBM per device.

v0:
```python
import jax
import jax.numpy as jnp
from jax import lax
from jax.sharding import PartitionSpec as P

ITERS = 2


EPS = 1e-06


def conj_apply(inputs, blocks):
    sparsity_layout = "sbp,bpq->sbq"
    real_part = jnp.einsum(
        sparsity_layout, inputs[0], blocks[:, 0], preferred_element_type=jnp.float32
    ) + jnp.einsum(sparsity_layout, inputs[1], blocks[:, 1], preferred_element_type=jnp.float32)
    imag_part = jnp.einsum(
        sparsity_layout, inputs[1], blocks[:, 0], preferred_element_type=jnp.float32
    ) - jnp.einsum(sparsity_layout, inputs[0], blocks[:, 1], preferred_element_type=jnp.float32)
    return (real_part, imag_part)


def plain_apply(factors, blocks):
    sparsity_layout = "fan,aun->fau"
    real_part = jnp.einsum(
        sparsity_layout, factors[0], blocks[:, 0], preferred_element_type=jnp.float32
    ) - jnp.einsum(sparsity_layout, factors[1], blocks[:, 1], preferred_element_type=jnp.float32)
    imag_part = jnp.einsum(
        sparsity_layout, factors[0], blocks[:, 1], preferred_element_type=jnp.float32
    ) + jnp.einsum(sparsity_layout, factors[1], blocks[:, 0], preferred_element_type=jnp.float32)
    return (real_part, imag_part)


def fetch_inputs(rounded_result, far_row_leaf, near_col_leaf, near_offset, leaf_size, leaves_here):
    rhs_count = rounded_result.shape[1]
    cluster_count = lax.axis_size("cluster")
    leaf_count = leaves_here * cluster_count
    gathered = lax.all_gather(rounded_result, ("cluster", "blk"), axis=2, tiled=True)
    leaves = gathered.reshape(2, rhs_count, leaf_count, leaf_size)
    near_row_leaf = (near_col_leaf + near_offset) % leaf_count
    far_input_vector = jnp.take(leaves, far_row_leaf, axis=2)
    near_in = jnp.take(leaves, near_row_leaf, axis=2)
    return (far_input_vector, near_in)


def adjoint(
    vector,
    far_row_factor,
    far_col_factor,
    far_rank,
    far_row_leaf,
    far_block_column_leaf,
    near_matrix,
    near_col_leaf,
    near_offset,
):
    leaf_size = far_row_factor.shape[2]
    rank_cap = far_row_factor.shape[3]
    rhs_count = vector.shape[1]
    segment_len = vector.shape[2] * lax.axis_size("blk")
    leaves_here = segment_len // leaf_size
    cluster_pos = lax.axis_index("cluster")
    rounded_result = vector.astype(jnp.bfloat16)
    far_input_vector, near_in = fetch_inputs(
        rounded_result, far_row_leaf, near_col_leaf, near_offset, leaf_size, leaves_here
    )
    coef_real, coef_imag = conj_apply(far_input_vector, far_row_factor)
    rank_mask = (jnp.arange(rank_cap)[None, :] < far_rank[:, None]).astype(jnp.float32)
    factors = jnp.stack([coef_real * rank_mask[None], coef_imag * rank_mask[None]]).astype(
        jnp.bfloat16
    )
    far_real, far_imag = plain_apply(factors, far_col_factor)
    near_real, near_imaginary_entries = conj_apply(near_in, near_matrix)
    out_real = jnp.concatenate([far_real, near_real], axis=1)
    out_imag = jnp.concatenate([far_imag, near_imaginary_entries], axis=1)
    local_cols = jnp.concatenate([far_block_column_leaf, near_col_leaf]) - cluster_pos * leaves_here
    onehot_table = (local_cols[:, None] == jnp.arange(leaves_here)[None, :]).astype(jnp.float32)
    sums_real = jnp.einsum("sbq,bl->slq", out_real, onehot_table, precision=lax.Precision.HIGHEST)
    sums_imag = jnp.einsum("sbq,bl->slq", out_imag, onehot_table, precision=lax.Precision.HIGHEST)
    segment = jnp.stack([sums_real, sums_imag]).reshape(2, rhs_count, segment_len)
    return lax.psum_scatter(segment, "blk", scatter_dimension=2, tiled=True)


def local_inner(left_side, right_side):
    real_part = jnp.sum(left_side[0] * right_side[0] + left_side[1] * right_side[1], axis=1)
    imag_part = jnp.sum(left_side[0] * right_side[1] - left_side[1] * right_side[0], axis=1)
    return jnp.stack([real_part, imag_part])


def body(
    rhs_block,
    far_row_factor,
    far_col_factor,
    far_rank,
    far_row_leaf,
    far_block_column_leaf,
    near_matrix,
    near_col_leaf,
    near_offset,
):
    total_panels = rhs_block.shape[2] * lax.axis_size("cluster") * lax.axis_size("blk")
    start_sum = lax.psum(jnp.sum(rhs_block * rhs_block, axis=(0, 2)), ("cluster", "blk"))
    start_scale = jnp.sqrt(start_sum / total_panels + EPS)
    krylov_basis = [rhs_block / start_scale[None, :, None]]
    coeffs = []
    for section_index in range(ITERS):
        applied = adjoint(
            krylov_basis[section_index],
            far_row_factor,
            far_col_factor,
            far_rank,
            far_row_leaf,
            far_block_column_leaf,
            near_matrix,
            near_col_leaf,
            near_offset,
        )
        local_sums = jnp.stack(
            [local_inner(krylov_basis[earlier], applied) for earlier in range(section_index + 1)]
        )
        correlations = lax.psum(local_sums, ("cluster", "blk"))
        correlations = correlations / total_panels
        reduced = applied
        for earlier in range(section_index + 1):
            previous = krylov_basis[earlier]
            real_part = correlations[earlier, 0]
            imag_part = correlations[earlier, 1]
            coeffs.append(real_part)
            coeffs.append(imag_part)
            mix_real = real_part[:, None] * previous[0] - imag_part[:, None] * previous[1]
            mix_imag = real_part[:, None] * previous[1] + imag_part[:, None] * previous[0]
            reduced = reduced - jnp.stack([mix_real, mix_imag])
        length_sq = (
            lax.psum(jnp.sum(reduced * reduced, axis=(0, 2)), ("cluster", "blk")) / total_panels
        )
        vector_length = jnp.sqrt(length_sq + EPS)
        coeffs.append(vector_length)
        krylov_basis.append(reduced / vector_length[None, :, None])
    return (krylov_basis[-1], jnp.stack(coeffs, axis=1))


def solution(mesh):
    placed = (
        P(None, None, ("cluster", "blk")),
        P(("cluster", "blk"), None, None, None),
        P(("cluster", "blk"), None, None, None),
        P(("cluster", "blk")),
        P(("cluster", "blk")),
        P(("cluster", "blk")),
        P(("cluster", "blk"), None, None, None),
        P(("cluster", "blk")),
        P(("cluster", "blk")),
    )
    return jax.shard_map(
        body,
        mesh=mesh,
        in_specs=placed,
        out_specs=(P(None, None, ("cluster", "blk")), P()),
        check_vma=False,
    )
```

profile of v0, /device:TPU:1, one launch (start us, length us, event | category | flops | bytes accessed | tf_op | source)
XLA Modules:
  0.0 588.2 jit_solution(4823159526641906132)
XLA Ops:
  7.2 0.9 multiply_reduce_fusion.2
  8.1 68.7 %psum.35 = f32[32]{0:T(128)S(1)} all-reduce(f32[32]{0:T(128)S(1)} %multiply_reduce_fusion.2), channel_id=1, replica_groups=mesh['cluster'=16,'blk'=8] {'cluster','blk'}, use_global_device_ids=true, to_apply=%region_1.0 | all-reduce | flops 32 | bytes 256 | tf_op jit(solution)/shard_map/psum | solution.py:102
  76.8 1.4 fusion.183
  78.3 0.8 add_subtract_fusion
  79.1 0.7 compare_and_fusion.1
  81.1 0.7 fusion.169
  81.8 57.5 %all-gather.3.cloned.1.call-done = bf16[2,32,16384]{2,1,0:T(8,128)(2,1)} async-done(((bf16[2,32,128]{2,1,0:T(8,128)(2,1)}), bf16[2,32,16384]{2,1,0:T(8,128)(2,1)}) %all-gather.3.cloned.1.call-update) | async-done | bytes 2097168 | tf_op jit(solution)/shard_map/all_gather | solution.py:38
  139.3 3.3 copy_bitcast_fusion.1
  142.6 2.4 gather_fusion.1
  145.1 1.2 fusion.152
  146.7 3.3 gather_fusion
  150.0 1.5 fusion.157
  151.5 2.3 fusion.20
  154.9 1.2 fusion.118
  157.8 1.5 copy-done.2
  159.3 1.2 fusion.6
  160.5 2.2 fusion.4
  162.7 1.2 fusion.67
  164.1 1.5 fusion.132
  165.6 3.1 fusion.73
  168.9 1.5 fusion.135
  170.4 0.7 pad_maximum_fusion.4
  171.2 26.8 %reduce-scatter.3.cloned.1.call-done = f32[2,32,128]{2,1,0:T(8,128)} async-done(((f32[2,32,1024]{2,1,0:T(8,128)}), f32[2,32,128]{2,1,0:T(8,128)}) %reduce-scatter.3.cloned.1.call-update) | async-done | bytes 32784 | tf_op jit(solution)/shard_map/reduce_scatter | solution.py:81
  198.1 0.8 add_reduce_fusion.2
  198.9 67.5 %psum.36 = f32[1,2,32]{2,1,0:T(2,128)S(1)} all-reduce(f32[1,2,32]{2,1,0:T(2,128)S(1)} %maximum_bitcast_fusion), channel_id=1, replica_groups=mesh['cluster'=16,'blk'=8] {'cluster','blk'}, use_global_device_ids=true, to_apply=%region_5.8 | all-reduce | flops 64 | bytes 512 | tf_op jit(solution)/shard_map/psum | solution.py:121
  266.5 0.9 multiply_reduce_fusion.1
  267.4 62.6 %psum.37 = f32[32]{0:T(128)S(1)} all-reduce(f32[32]{0:T(128)S(1)} %multiply_reduce_fusion.1), channel_id=1, replica_groups=mesh['cluster'=16,'blk'=8] {'cluster','blk'}, use_global_device_ids=true, to_apply=%region_7.10 | all-reduce | flops 32 | bytes 256 | tf_op jit(solution)/shard_map/psum | solution.py:134
  329.9 1.4 fusion.182
  331.6 61.6 %all-gather.5.cloned.1.call-done = bf16[2,32,16384]{2,1,0:T(8,128)(2,1)} async-done(((bf16[2,32,128]{2,1,0:T(8,128)(2,1)}), bf16[2,32,16384]{2,1,0:T(8,128)(2,1)}) %all-gather.5.cloned.1.call-update) | async-done | bytes 2097168 | tf_op jit(solution)/shard_map/all_gather | solution.py:38
  393.2 3.3 copy_bitcast_fusion
  396.5 3.0 gather_fusion.3
  399.5 2.3 gather_fusion.2
  401.9 1.2 fusion.166
  404.0 1.2 copy-done.1
  408.0 1.5 copy-done.3
  409.5 1.2 fusion.2
  411.4 1.2 fusion
  412.6 1.2 fusion.79
  413.9 1.5 fusion.138
  415.5 2.8 fusion.85
  418.4 1.5 fusion.141
  419.9 0.7 pad_maximum_fusion.5
  420.7 26.9 %reduce-scatter.5.cloned.1.call-done = f32[2,32,128]{2,1,0:T(8,128)} async-done(((f32[2,32,1024]{2,1,0:T(8,128)}), f32[2,32,128]{2,1,0:T(8,128)}) %reduce-scatter.5.cloned.1.call-update) | async-done | bytes 32784 | tf_op jit(solution)/shard_map/reduce_scatter | solution.py:81
  447.6 0.9 add_reduce_fusion.1
  448.5 67.5 %psum.38 = f32[2,2,32]{2,1,0:T(2,128)S(1)} all-reduce(f32[2,2,32]{2,1,0:T(2,128)S(1)} %pad_maximum_fusion.6), channel_id=1, replica_groups=mesh['cluster'=16,'blk'=8] {'cluster','blk'}, use_global_device_ids=true, to_apply=%region_13.16 | all-reduce | flops 128 | bytes 1024 | tf_op jit(solution)/shard_map/psum | solution.py:121
  516.1 0.9 multiply_reduce_fusion
  517.0 62.6 %psum.39 = f32[32]{0:T(128)S(1)} all-reduce(f32[32]{0:T(128)S(1)} %multiply_reduce_fusion), channel_id=1, replica_groups=mesh['cluster'=16,'blk'=8] {'cluster','blk'}, use_global_device_ids=true, to_apply=%region_15.18 | all-reduce | flops 32 | bytes 256 | tf_op jit(solution)/shard_map/psum | solution.py:134
  580.2 1.4 broadcast_divide_fusion
  (60 shorter events, 11.1 us)
Async XLA Ops:
  7.2 132.1 %all-gather.3.cloned.1.call-start = ((), (), s32[]{:S(2)}) async-start(), calls=%async_computation.2 | async-start | bytes 2113536 | tf_op jit(solution)/shard_map/all_gather | solution.py:38
  78.3 119.8 %reduce-scatter.3.cloned.1.call-start = ((), (), s32[]{:S(2)}) async-start(), calls=%async_computation.3 | async-start | bytes 294912 | tf_op jit(solution)/shard_map/reduce_scatter | solution.py:81
  142.6 2.5 copy-start.4
  150.0 3.8 copy-start
  153.8 1.0 copy-start.5
  157.1 2.2 copy-start.2
  165.6 3.1 copy-start.6
  171.2 222.0 %all-gather.5.cloned.1.call-start = ((), (), s32[]{:S(2)}) async-start(), calls=%async_computation.4 | async-start | bytes 2113536 | tf_op jit(solution)/shard_map/all_gather | solution.py:38
  331.4 116.2 %reduce-scatter.5.cloned.1.call-start = ((), (), s32[]{:S(2)}) async-start(), calls=%async_computation.5 | async-start | bytes 294912 | tf_op jit(solution)/shard_map/reduce_scatter | solution.py:81
  403.0 2.2 copy-start.1
  407.3 2.2 copy-start.3
Sparse Core Ops, SparseCore 0:
  78.4 60.8 all-gather.2
  171.3 26.7 reduce-scatter.2
  331.5 61.6 all-gather.4
  420.8 26.7 reduce-scatter.4
where the time goes:
time: 590 us; the launch traced here: 588 us
  blocking collectives  329 us (56%)
  waiting for transfers between devices  173 us (29%)
  matrix products  31.8 us (5%)
  local copies, waits for them, and re-layouts  23 us (4%)
  other arithmetic  17.4 us (3%)
  between operations  14 us (2%)
    psum x2, blocking collectives, body(): correlations = lax.psum(local_sums, ('cluster', 'blk'))  135 us
    psum x2, blocking collectives, body(): lax.psum(jnp.sum(reduced * reduced, axis=(0, 2)), ('cluster', 'blk'))  125 us
    all_gather x2, waiting for transfers between devices, fetch_inputs(): lax.all_gather(rounded_result, ('cluster', 'blk'), axis=2, tiled=True)  119 us
    psum x1, blocking collectives, body(): lax.psum(jnp.sum(rhs_block * rhs_block, axis=(0, 2)), ('cluster', 'blk'))  68.7 us
    reduce_scatter x2, waiting for transfers between devices, adjoint(): return lax.psum_scatter(segment, 'blk', scatter_dimension=2, tiled=True)  53.7 us
  transfers between devices with their start and end apart: 4, of which 4 were waited for; matrix products, arithmetic and copies ran while one was open for 1% of the time, Pallas kernels for 0%

commit v1 on v0

v1 whole, which is shorter than its diff:
```python
import jax
import jax.numpy as jnp
from jax import lax
from jax.experimental import pallas as pl
from jax.experimental.pallas import tpu as pltpu
from jax.sharding import PartitionSpec as P

MESH = pl.DeviceIdType.MESH
F32, BF16, I32 = jnp.float32, jnp.bfloat16, jnp.int32
EPS = 1e-06
SIDE = 4
BLK = 8
CLUSTERS = 16
LEAVES = 128
LEAF = 128
RHS = 32
ROWS = 2 * RHS
FAR = 64
NEAR = 32
PANELS = LEAVES * LEAF
DOWN, UP = 2.0**-40, 2.0**40

FB, FLEAF, FRANK, CB, CPOS, CKEEP, CLAST, CCOUNT, NB, NLEAF, NKEEP, NLAST, NCOUNT = range(13)


def dot_kn(a, b):
    return lax.dot_general(a, b, (((1,), (0,)), ((), ())), preferred_element_type=F32)


def dot_nk(a, b):
    return lax.dot_general(a, b, (((1,), (1,)), ((), ())), preferred_element_type=F32)


def conj_apply(x, w):
    turned = jnp.concatenate([x[RHS:], -x[:RHS]], axis=0)
    return dot_kn(jnp.concatenate([x, turned], axis=1), w)


def plain_apply(t, w):
    both = dot_nk(t, w)
    real, imag = both[:, :LEAF], both[:, LEAF:]
    return jnp.concatenate([real[:RHS] - imag[RHS:], real[RHS:] + imag[:RHS]], axis=0)


def lane_sum(a):
    return jnp.sum(a, axis=1, keepdims=True)


def twice(a):
    return jnp.concatenate([a, a], axis=0)


class Net:
    def __init__(self, send_sem, recv_sem):
        self.send_sem, self.recv_sem, self.count, self.open = send_sem, recv_sem, 0, []

    def put(self, src, dst, device):
        i = self.count
        self.count += 1
        copy = pltpu.make_async_remote_copy(
            src_ref=src,
            dst_ref=dst,
            send_sem=self.send_sem.at[i],
            recv_sem=self.recv_sem.at[i],
            device_id=device,
            device_id_type=MESH,
        )
        copy.start()
        self.open.append(copy)
        return i

    def got(self, i, land, device):
        pltpu.make_async_remote_copy(
            src_ref=land,
            dst_ref=land,
            send_sem=self.send_sem.at[i],
            recv_sem=self.recv_sem.at[i],
            device_id=device,
            device_id_type=MESH,
        ).wait_recv()

    def sent(self):
        for copy in self.open:
            copy.wait_send()
        self.open = []


N_SEMS = 256


def sort_order(key_row, key_col, size):
    return jnp.sum(jnp.where(key_row < key_col, 1, 0), axis=1, keepdims=True).astype(I32)


def in_order(place, values, lanes):
    return jnp.sum(jnp.where(place == lanes, values, 0), axis=0, keepdims=True).astype(I32)


def column(row, size, lanes, subs):
    return jnp.sum(jnp.where(lanes == subs, jnp.broadcast_to(row, (size, LEAF)), 0), axis=1, keepdims=True).astype(I32)


def padded(ref, size):
    return jnp.concatenate([ref[...].reshape(1, size), jnp.zeros((1, LEAF - size), I32)], axis=1)


def build_table(table, rank_v, row_v, col_v, ncol_v, noff_v, cluster, y, z):
    lanes = lax.broadcasted_iota(I32, (FAR, LEAF), 1)
    subs = lax.broadcasted_iota(I32, (FAR, LEAF), 0)
    index = lax.broadcasted_iota(I32, (FAR, 1), 0)
    lane_row = lax.broadcasted_iota(I32, (1, LEAF), 1)
    big = 1 << 20

    def keys(values, size):
        row = jnp.where(lane_row < size, values * size + lane_row, big)
        return row

    row_leaf = padded(row_v, FAR)
    seg = row_leaf >> 3
    away = (((seg >> 2) - y + SIDE) & 3) * SIDE + (((seg & 3) - z + SIDE) & 3)
    key1 = keys(away * BLK + (row_leaf & 7), FAR)
    place1 = sort_order(key1, column(key1, FAR, lanes, subs), FAR)
    leaf_col = column(row_leaf, FAR, lanes, subs)
    rank_col = column(padded(rank_v, FAR), FAR, lanes, subs)
    table[FB : FB + 1] = in_order(place1, index, lanes)
    table[FLEAF : FLEAF + 1] = in_order(place1, leaf_col, lanes)
    table[FRANK : FRANK + 1] = in_order(place1, rank_col, lanes)

    def columns(values, size, lanes, subs, index):
        key = keys(values, size)
        place = sort_order(key, column(key, size, lanes, subs), size)
        own = column(values, size, lanes, subs)
        valid = lanes < size
        earlier = jnp.sum(jnp.where(valid & (values == own) & (lanes < subs), 1, 0), axis=1, keepdims=True)
        keep = jnp.where(earlier > 0, 1, 0).astype(I32)
        upto = jnp.sum(jnp.where(own <= lanes, 1, 0), axis=0, keepdims=True).astype(I32)
        here = jnp.sum(jnp.where(own == lanes, 1, 0), axis=0, keepdims=True).astype(I32)
        return place, keep, jnp.maximum(upto - 1, 0), here

    local = padded(col_v, FAR) - cluster * BLK
    place2, keep2, last2, here2 = columns(local, FAR, lanes, subs, index)
    table[CB : CB + 1] = in_order(place2, index, lanes)
    table[CPOS : CPOS + 1] = in_order(place2, place1, lanes)
    table[CKEEP : CKEEP + 1] = in_order(place2, keep2, lanes)
    table[CLAST : CLAST + 1] = last2
    table[CCOUNT : CCOUNT + 1] = here2

    lanes, subs, index = lanes[:NEAR], subs[:NEAR], index[:NEAR]
    ncol = padded(ncol_v, NEAR)
    place3, keep3, last3, here3 = columns(ncol - cluster * BLK, NEAR, lanes, subs, index)
    source = (ncol + padded(noff_v, NEAR) + LEAVES) & (LEAVES - 1)
    table[NB : NB + 1] = in_order(place3, index, lanes)
    table[NLEAF : NLEAF + 1] = in_order(place3, column(source, NEAR, lanes, subs), lanes)
    table[NKEEP : NKEEP + 1] = in_order(place3, keep3, lanes)
    table[NLAST : NLAST + 1] = last3
    table[NCOUNT : NCOUNT + 1] = here3


def kernel(
    rhs_h, u_h, v_h, rank_h, row_h, col_h, near_h, ncol_h, noff_h,
    out_ref, hess_ref,
    u, v, near, rank_v, row_v, col_v, ncol_v, noff_v, table, idx,
    r32, w32, g0, g1, t, far_run, near_run, part0, part1, rs0, rs1,
    ay, az, by, bz, cx, cy, cz,
    load_sem, send_sem, recv_sem,
):
    cluster, blk = lax.axis_index("cluster"), lax.axis_index("blk")
    y, z = cluster // SIDE, cluster % SIDE
    core = blk % 2
    net = Net(send_sem, recv_sem)

    def dev_blk(d):
        return (cluster, (blk + d) % BLK)

    def dev_y(d):
        return (((y + d) % SIDE) * SIDE + z, blk)

    def dev_z(d):
        return (y * SIDE + (z + d) % SIDE, blk)

    mate = (cluster, blk + 1 - 2 * core)

    barrier = pltpu.get_barrier_semaphore()
    partners = [dev_blk(d) for d in range(1, BLK)]
    partners += [dev_y(d) for d in range(1, SIDE)] + [dev_z(d) for d in range(1, SIDE)]
    for partner in partners:
        pl.semaphore_signal(barrier, inc=1, device_id=partner, device_id_type=MESH)

    loads = [
        (rhs_h, r32.at[blk]), (rank_h, rank_v), (row_h, row_v), (col_h, col_v),
        (ncol_h, ncol_v), (noff_h, noff_v), (u_h, u), (near_h, near), (v_h, v),
    ]
    loads = [pltpu.make_async_copy(src, dst, load_sem.at[i]) for i, (src, dst) in enumerate(loads)]
    for load in loads:
        load.start()
    for load in loads[:6]:
        load.wait()
    pl.semaphore_wait(barrier, len(partners))

    def blk_start(buf):
        return [net.put(buf.at[blk], buf.at[blk], dev_blk(d)) for d in range(1, BLK)]

    def blk_wait(buf, ids):
        for d, i in zip(range(1, BLK), ids):
            net.got(i, buf.at[(blk - d + BLK) % BLK], dev_blk(d))

    def y_start(buf):
        return [net.put(buf.at[y], buf.at[y], dev_y(d)) for d in range(1, SIDE)]

    def y_wait(buf, ids):
        for d, i in zip(range(1, SIDE), ids):
            net.got(i, buf.at[(y - d + SIDE) % SIDE], dev_y(d))

    def z_start(buf):
        return [net.put(buf.at[z], buf.at[z], dev_z(d)) for d in range(1, SIDE)]

    def z_wait(buf, ids):
        for d, i in zip(range(1, SIDE), ids):
            net.got(i, buf.at[(z - d + SIDE) % SIDE], dev_z(d))

    def plane_sum(value, buf_y, buf_z):
        buf_y[y] = value
        y_wait(buf_y, y_start(buf_y))
        buf_z[z] = (buf_y[0] + buf_y[1]) + (buf_y[2] + buf_y[3])
        z_wait(buf_z, z_start(buf_z))
        return (buf_z[0] + buf_z[1]) + (buf_z[2] + buf_z[3])

    def pack(values):
        lanes = lax.broadcasted_iota(I32, (RHS, LEAF), 1)
        packed = jnp.zeros((RHS, LEAF), F32)
        for i, value in enumerate(values):
            packed = jnp.where(lanes == i, value, packed)
        return packed

    def gather(g):
        def piece(yy, zz, c, j):
            return g.at[pl.ds((yy * SIDE + zz) * BLK + SIDE * c + 2 * j, 2)]

        def at(p, d):
            return (p + d + SIDE) % SIDE

        forwards = []
        second = {}

        def forward(yy_d, zz_d, j):
            src = piece(at(y, -yy_d), at(z, -zz_d), core, j)
            forwards.append((net.put(src, src, mate), yy_d, zz_d, j))

        own = [piece(y, z, core, j) for j in range(2)]
        first = []
        for d in range(1, SIDE):
            first.append((net.put(own[0], own[0], dev_y(d)), d, 0))
            first.append((net.put(own[1], own[1], dev_z(d)), d, 1))
        for d in range(1, SIDE):
            second[0, d, 0] = net.put(own[0], own[0], dev_z(d))
            second[d, 0, 1] = net.put(own[1], own[1], dev_y(d))
        for i, d, j in first:
            yy_d, zz_d = (d, 0) if j == 0 else (0, d)
            land = piece(at(y, -yy_d), at(z, -zz_d), core, j)
            net.got(i, land, dev_y(d) if j == 0 else dev_z(d))
            for e in range(1, SIDE):
                if j == 0:
                    second[d, e, 0] = net.put(land, land, dev_z(e))
                else:
                    second[e, d, 1] = net.put(land, land, dev_y(e))
            forward(yy_d, zz_d, j)
        for (yy_d, zz_d, j), i in second.items():
            land = piece(at(y, -yy_d), at(z, -zz_d), core, j)
            net.got(i, land, dev_z(zz_d) if j == 0 else dev_y(yy_d))
            forward(yy_d, zz_d, j)
        for i, yy_d, zz_d, j in forwards:
            net.got(i, piece(at(y, -yy_d), at(z, -zz_d), 1 - core, j), mate)

    lane = lax.broadcasted_iota(I32, (ROWS, LEAF), 1)

    def apply_all(g, part):
        def row_step(j, carry):
            x = g[idx[FLEAF, j]]
            c = conj_apply(x, u[idx[FB, j]])
            t[j] = jnp.where(lane < idx[FRANK, j], c, 0.0).astype(BF16)
            return carry

        lax.fori_loop(0, FAR, row_step, 0, unroll=8)

        def near_step(j, total):
            term = conj_apply(g[idx[NLEAF, j]], near[idx[NB, j]])
            total = jnp.where(idx[NKEEP, j] > 0, total, 0.0) + term
            near_run[j] = total
            return total

        zero = jnp.zeros((ROWS, LEAF), F32)
        lax.fori_loop(0, NEAR, near_step, zero, unroll=8)

        def col_step(j, total):
            term = plain_apply(t[idx[CPOS, j]], v[idx[CB, j]])
            total = jnp.where(idx[CKEEP, j] > 0, total, 0.0) + term
            far_run[j] = total
            return total

        lax.fori_loop(0, FAR, col_step, zero, unroll=8)
        for l in range(BLK):
            far_sum = jnp.where(idx[CCOUNT, l] > 0, far_run[idx[CLAST, l]], 0.0)
            near_sum = jnp.where(idx[NCOUNT, l] > 0, near_run[idx[NLAST, l]], 0.0)
            part[l] = far_sum + near_sum

    def reduce_scatter(part, rs):
        ids = []
        for d in range(1, BLK):
            ids.append(net.put(part.at[(blk + d) % BLK], rs.at[blk], dev_blk(d)))
        total = part[blk]
        blk_wait(rs, ids)
        for d in range(1, BLK):
            total = total + rs[(blk - d + BLK) % BLK]
        return total

    def re(a):
        return a[:RHS]

    def im(a):
        return a[RHS:]

    ids = blk_start(r32)
    build_table(table, rank_v, row_v, col_v, ncol_v, noff_v, cluster, y, z)
    to_scalar = pltpu.make_async_copy(table, idx, load_sem.at[len(loads)])
    to_scalar.start()
    blk_wait(r32, ids)
    squares = jnp.zeros((RHS, LEAF), F32)
    for l in range(BLK):
        a = r32[l]
        squares = squares + (re(a) * re(a) + im(a) * im(a))
    total = plane_sum(pack([lane_sum(squares)]), ay, az)
    net.sent()
    scale = twice(jnp.sqrt(total[:, 0:1] / PANELS + EPS))
    for l in range(BLK):
        q = r32[l] / scale
        r32[l] = q
        g0[cluster * BLK + l] = q.astype(BF16)

    for load in loads[6:]:
        load.wait()
    to_scalar.wait()
    gather(g0)
    apply_all(g0, part0)
    w32[blk] = reduce_scatter(part0, rs0)
    blk_wait(w32, blk_start(w32))
    zero = jnp.zeros((RHS, LEAF), F32)
    hr, hi, ww, qq = zero, zero, zero, zero
    for l in range(BLK):
        q, w = r32[l], w32[l]
        hr = hr + (re(q) * re(w) + im(q) * im(w))
        hi = hi + (re(q) * im(w) - im(q) * re(w))
        ws = w * DOWN
        ww = ww + (re(ws) * re(ws) + im(ws) * im(ws))
        qq = qq + (re(q) * re(q) + im(q) * im(q))
    total = plane_sum(pack([lane_sum(a) for a in (hr, hi, ww, qq)]), by, bz) / PANELS
    h00r, h00i, ww, g00 = (total[:, i : i + 1] for i in range(4))
    sr, si = h00r * DOWN, h00i * DOWN
    left = ww - (sr * sr + si * si) * (2.0 - g00)
    net.sent()
    h10 = jnp.sqrt(jnp.maximum(left, 0.0) * UP * UP + EPS)
    for l in range(BLK):
        q, w = r32[l], w32[l]
        real = re(w) - (h00r * re(q) - h00i * im(q))
        imag = im(w) - (h00r * im(q) + h00i * re(q))
        q1 = jnp.concatenate([real / h10, imag / h10], axis=0)
        w32[l] = q1
        g1[cluster * BLK + l] = q1.astype(BF16)

    gather(g1)
    apply_all(g1, part1)
    q0, q1 = r32[blk], w32[blk]
    w = reduce_scatter(part1, rs1)
    ws = w * DOWN

    def inner(a, b):
        return (
            lane_sum(re(a) * re(b) + im(a) * im(b)),
            lane_sum(re(a) * im(b) - im(a) * re(b)),
        )

    values = [*inner(q0, w), *inner(q1, w), inner(ws, ws)[0], inner(q1, q1)[0], *inner(q0, q1)]
    cx[blk] = pack(values)
    blk_wait(cx, blk_start(cx))
    total = cx[0]
    for l in range(1, BLK):
        total = total + cx[l]
    total = plane_sum(total, cy, cz) / PANELS
    ar, ai, br, bi, ww, g11, cr, ci = (total[:, i : i + 1] for i in range(8))
    real = re(w) - (ar * re(q0) - ai * im(q0)) - (br * re(q1) - bi * im(q1))
    imag = im(w) - (ar * im(q0) + ai * re(q0)) - (br * im(q1) + bi * re(q1))
    sar, sai, sbr, sbi = ar * DOWN, ai * DOWN, br * DOWN, bi * DOWN
    left = ww - (sar * sar + sai * sai) * (2.0 - g00) - (sbr * sbr + sbi * sbi) * (2.0 - g11)
    pr, pi = sar * sbr + sai * sbi, sar * sbi - sai * sbr
    left = left + 2.0 * (pr * cr - pi * ci)
    h21 = jnp.sqrt(jnp.maximum(left, 0.0) * UP * UP + EPS)
    out_ref[...] = jnp.concatenate([real / h21, imag / h21], axis=0)
    hess_ref[...] = pack([h00r, h00i, h10, ar, ai, br, bi, h21])[:, :8]
    net.sent()


def body(rhs, u, v, rank, row, col, near, ncol, noff):
    hbm = pl.BlockSpec(memory_space=pl.ANY)
    vmem = pl.BlockSpec(memory_space=pltpu.VMEM)
    seg = pltpu.VMEM((BLK, ROWS, LEAF), F32)
    vec = pltpu.VMEM((LEAVES, ROWS, LEAF), BF16)
    small = pltpu.VMEM((SIDE, RHS, LEAF), F32)
    out, hess = pl.pallas_call(
        kernel,
        out_shape=(
            jax.ShapeDtypeStruct((ROWS, LEAF), F32),
            jax.ShapeDtypeStruct((RHS, 8), F32),
        ),
        in_specs=[hbm] * 9,
        out_specs=(vmem, vmem),
        scratch_shapes=[
            pltpu.VMEM((FAR, 2 * LEAF, LEAF), BF16),
            pltpu.VMEM((FAR, 2 * LEAF, LEAF), BF16),
            pltpu.VMEM((NEAR, 2 * LEAF, LEAF), BF16),
            pltpu.VMEM((FAR,), I32),
            pltpu.VMEM((FAR,), I32),
            pltpu.VMEM((FAR,), I32),
            pltpu.VMEM((NEAR,), I32),
            pltpu.VMEM((NEAR,), I32),
            pltpu.VMEM((16, LEAF), I32),
            pltpu.SMEM((16, LEAF), I32),
            seg, seg, vec, vec,
            pltpu.VMEM((FAR, ROWS, LEAF), BF16),
            pltpu.VMEM((FAR, ROWS, LEAF), F32),
            pltpu.VMEM((NEAR, ROWS, LEAF), F32),
            seg, seg, seg, seg,
            small, small, small, small,
            pltpu.VMEM((BLK, RHS, LEAF), F32), small, small,
            pltpu.SemaphoreType.DMA((16,)),
            pltpu.SemaphoreType.DMA((N_SEMS,)),
            pltpu.SemaphoreType.DMA((N_SEMS,)),
        ],
        compiler_params=pltpu.CompilerParams(
            collective_id=0, has_side_effects=True, vmem_limit_bytes=48 * 2**20
        ),
    )(
        rhs.reshape(ROWS, LEAF),
        u.reshape(FAR, 2 * LEAF, LEAF),
        v.reshape(FAR, 2 * LEAF, LEAF),
        rank, row, col,
        near.reshape(NEAR, 2 * LEAF, LEAF),
        ncol, noff,
    )
    return out.reshape(2, RHS, LEAF), hess


def solution(mesh):
    split = P(("cluster", "blk"))
    vector = P(None, None, ("cluster", "blk"))
    blocks = P(("cluster", "blk"), None, None, None)
    return jax.shard_map(
        body,
        mesh=mesh,
        in_specs=(vector, blocks, blocks, split, split, split, blocks, split, split),
        out_specs=(vector, P()),
        check_vma=False,
    )
```

time: 590 us -> 97.3 us (0.16)
  blocking collectives: 329 us -> 0 us
  waiting for transfers between devices: 173 us -> 0 us
  Pallas kernels: 0 us -> 88.8 us
  matrix products: 31.8 us -> 0 us
  other arithmetic: 17.4 us -> 0 us
  local copies, waits for them, and re-layouts: 23 us -> 6.89 us
  between operations: 14 us -> 0.66 us
    psum x5 -> x0, blocking collectives: 329 us -> none  [the longest x2 135 us: body(): correlations = lax.psum(local_sums, ('cluster', 'blk'))]
    all_gather x2 -> x0, waiting for transfers between devices: 119 us -> none  [fetch_inputs(): lax.all_gather(rounded_result, ('cluster', 'blk'), axis=2, tiled=True)]
    pallas_call x0 -> x1, Pallas kernels: none -> 88.8 us  [body(): pl.pallas_call(kernel, out_shape=(jax.ShapeDtypeStruct((ROWS, LEAF), F32)...]
    reduce_scatter x2 -> x0, waiting for transfers between devices: 53.7 us -> none  [adjoint(): return lax.psum_scatter(segment, 'blk', scatter_dimension=2, tiled=True)]
    dot_general x28 -> x0, matrix products: 31.8 us -> none  [the longest x2 5.9 us: plain_apply(): jnp.einsum(sparsity_layout, factors[1], blocks[:, 0], preferred_element_t...]
    gather x4 -> x0, local copies, waits for them, and re-layouts: 11 us -> none  [the longest x2 5.6 us: fetch_inputs(): far_input_vector = jnp.take(leaves, far_row_leaf, axis=2)]
    reshape x2 -> x0, local copies, waits for them, and re-layouts: 6.6 us -> none  [fetch_inputs(): leaves = gathered.reshape(2, rhs_count, leaf_count, leaf_size)]
  transfers between devices with their start and end apart: 4 -> 0, of which waited for: 4 -> 0; matrix products, arithmetic and copies ran while one was open for 1% -> 0% of each run, Pallas kernels for 0% -> 0%
where the time goes in v1:
time: 97.3 us; the launch traced here: 96.3 us
  Pallas kernels  88.8 us (91%)
  local copies, waits for them, and re-layouts  6.89 us (7%)
    pallas_call x1, Pallas kernels, body(): pl.pallas_call(kernel, out_shape=(jax.ShapeDtypeStruct((ROWS, LEAF), F32)...  88.8 us
    unnamed x16, local copies, waits for them, and re-layouts  6.89 us

profile of v1, /device:TPU:1, one launch (start us, length us, event | category | flops | bytes accessed | tf_op | source)
XLA Modules:
  0.0 96.3 jit_solution(2506444147114410703)
XLA Ops:
  0.6 0.0 copy-start
  0.6 1.6 %copy-done = bf16[32,2,128,128]{3,2,1,0:T(8,128)(2,1)S(1)} copy-done((bf16[32,2,128,128]{3,2,1,0:T(8,128)(2,1)S(1)}, bf16[32,2,128,128]{3,2,1,0:T(8,128)(2,1)}, u32[]{:S(2)}) %copy-start) | copy-done | bytes 2097176
  2.2 0.0 copy-start.1
  2.2 0.8 copy-done.1
  3.0 0.0 copy-start.2
  3.0 0.7 copy-done.2
  3.6 0.0 copy-start.3
  3.6 0.7 copy-done.3
  4.3 0.0 copy-start.4
  4.3 0.7 copy-done.4
  5.0 0.0 copy-start.5
  5.0 0.7 copy-done.5
  5.6 0.0 copy-start.6
  5.6 0.7 copy-done.6
  6.3 88.8 %shard_map.104 = (f32[64,128]{1,0:T(8,128)S(1)}, f32[32,8]{1,0:T(8,128)S(1)}) custom-call(f32[64,128]{1,0:T(8,128)S(1)} %bitcast.6, bf16[64,256,128]{2,1,0:T(8,128)(2,1)} %bitcast.8, bf16[64,256,128]{2,1,0:T(8,128)(2,1)} %bitcast.9, s32[64]{0:T(128)S(1)} %copy-done.2, s32[64]{0:T(128)S(1)} %copy-done.3, s32[64]{0:T(128)S(1)} %copy-done.4, ...), custom_call_target="tpu_custom_call" | custom-call | tf_op jit(solution)/shard_map/pallas_call | solution.py:407
  95.0 0.7 copy.11
  95.7 0.6 copy.13
Async XLA Ops:
  0.6 1.6 %copy-start = (bf16[32,2,128,128]{3,2,1,0:T(8,128)(2,1)S(1)}, bf16[32,2,128,128]{3,2,1,0:T(8,128)(2,1)}, u32[]{:S(2)}) copy-start(bf16[32,2,128,128]{3,2,1,0:T(8,128)(2,1)} %param.15) | copy-start | bytes 6291460
  2.2 0.8 copy-start.1
  3.0 0.7 copy-start.2
  3.6 0.7 copy-start.3
  4.3 0.7 copy-start.4
  5.0 0.7 copy-start.5
  5.6 0.7 copy-start.6

commit v2 on v1

v2 whole, which is shorter than its diff:
```python
import jax
import jax.numpy as jnp
from jax import lax
from jax.experimental import pallas as pl
from jax.experimental.pallas import tpu as pltpu
from jax.sharding import PartitionSpec as P

MESH = pl.DeviceIdType.MESH
F32, BF16, I32 = jnp.float32, jnp.bfloat16, jnp.int32
EPS = 1e-06
VMEM_BYTES = 63 * 2**20
SIDE = 4
BLK = 8
CLUSTERS = 16
LEAVES = 128
LEAF = 128
RHS = 32
ROWS = 2 * RHS
FAR = 64
NEAR = 32
PANELS = LEAVES * LEAF
DOWN, UP = 2.0**-40, 2.0**40
FIRST = 36
AXES = ("z", "y", "x")
ROW_CUT = (
    {"z": (0, 32), "y": (32, 16), "x": (48, 16)},
    {"z": (0, 16), "y": (16, 32), "x": (48, 16)},
)

FB, FLEAF, FRANK, CB, CPOS, CKEEP, CLAST, CCOUNT, NB, NLEAF, NKEEP, NLAST, NCOUNT = range(13)


def dot_kn(a, b):
    return lax.dot_general(a, b, (((1,), (0,)), ((), ())), preferred_element_type=F32)


def dot_nk(a, b):
    return lax.dot_general(a, b, (((1,), (1,)), ((), ())), preferred_element_type=F32)


def re(a):
    a = a.reshape(a.shape[0] // 16, 2, 8, LEAF)
    return a[:, 0].reshape(-1, LEAF)


def im(a):
    a = a.reshape(a.shape[0] // 16, 2, 8, LEAF)
    return a[:, 1].reshape(-1, LEAF)


def join(real, imag):
    real, imag = real.reshape(-1, 1, 8, LEAF), imag.reshape(-1, 1, 8, LEAF)
    return jnp.concatenate([real, imag], axis=1).reshape(-1, LEAF)


def conj_apply(x, w):
    wide = x.astype(F32)
    turned = join(im(wide), -re(wide)).astype(BF16)
    return dot_kn(jnp.concatenate([x, turned], axis=1), w)


def plain_apply(t, w):
    both = dot_nk(t, w)
    real, imag = both[:, :LEAF], both[:, LEAF:]
    return join(re(real) - im(imag), im(real) + re(imag))


def pack(values):
    rows = []
    zero = jnp.zeros((RHS, LEAF), F32)
    for i in range(0, len(values), 4):
        four = values[i : i + 4]
        four = jnp.concatenate(four + [zero] * (4 - len(four)), axis=0)
        rows.append(jnp.sum(four.T, axis=0, keepdims=True))
    rows.append(jnp.zeros((8 - len(rows), LEAF), F32))
    return jnp.concatenate(rows, axis=0)


def unpack(tile, count):
    values = []
    for i in range(0, count, 4):
        square = jnp.broadcast_to(tile[i // 4 : i // 4 + 1], (LEAF, LEAF)).T
        values += [square[RHS * k : RHS * k + RHS] for k in range(4)]
    return values[:count]


def sort_order(key_row, key_col):
    return jnp.sum(jnp.where(key_row < key_col, 1, 0), axis=1, keepdims=True).astype(I32)


def in_order(place, values, lanes):
    return jnp.sum(jnp.where(place == lanes, values, 0), axis=0, keepdims=True).astype(I32)


def column(row, size, lanes, subs):
    return jnp.sum(jnp.where(lanes == subs, jnp.broadcast_to(row, (size, LEAF)), 0), axis=1, keepdims=True).astype(I32)


def padded(ref, size):
    return jnp.concatenate([ref[...].reshape(1, size), jnp.zeros((1, LEAF - size), I32)], axis=1)


def build_table(table, rank_v, row_v, col_v, ncol_v, noff_v, cluster, y, z):
    lanes = lax.broadcasted_iota(I32, (FAR, LEAF), 1)
    subs = lax.broadcasted_iota(I32, (FAR, LEAF), 0)
    index = lax.broadcasted_iota(I32, (FAR, 1), 0)
    lane_row = lax.broadcasted_iota(I32, (1, LEAF), 1)
    big = 1 << 20

    def keys(values, size):
        return jnp.where(lane_row < size, values * size + lane_row, big)

    row_leaf = padded(row_v, FAR)
    seg = row_leaf >> 3
    away_y = ((seg >> 2) - y + SIDE) & 3
    away_z = ((seg & 3) - z + SIDE) & 3
    late = jnp.where((away_y == 2) | (away_z == 2), 1, 0)
    key1 = keys(late, FAR)
    place1 = sort_order(key1, column(key1, FAR, lanes, subs))
    leaf_col = column(row_leaf, FAR, lanes, subs)
    rank_col = column(padded(rank_v, FAR), FAR, lanes, subs)
    table[FB : FB + 1] = in_order(place1, index, lanes)
    table[FLEAF : FLEAF + 1] = in_order(place1, leaf_col, lanes)
    table[FRANK : FRANK + 1] = in_order(place1, rank_col, lanes)

    def columns(values, size, lanes, subs):
        key = keys(values, size)
        place = sort_order(key, column(key, size, lanes, subs))
        own = column(values, size, lanes, subs)
        earlier = jnp.sum(jnp.where((values == own) & (lanes < subs), 1, 0), axis=1, keepdims=True)
        keep = jnp.where(earlier > 0, 1, 0).astype(I32)
        upto = jnp.sum(jnp.where(own <= lanes, 1, 0), axis=0, keepdims=True).astype(I32)
        here = jnp.sum(jnp.where(own == lanes, 1, 0), axis=0, keepdims=True).astype(I32)
        return place, keep, jnp.maximum(upto - 1, 0), here

    local = late * BLK + padded(col_v, FAR) - cluster * BLK
    place2, keep2, last2, here2 = columns(local, FAR, lanes, subs)
    table[CB : CB + 1] = in_order(place2, index, lanes)
    table[CPOS : CPOS + 1] = in_order(place2, place1, lanes)
    table[CKEEP : CKEEP + 1] = in_order(place2, keep2, lanes)
    table[CLAST : CLAST + 1] = last2
    table[CCOUNT : CCOUNT + 1] = here2

    lanes, subs, index = lanes[:NEAR], subs[:NEAR], index[:NEAR]
    ncol = padded(ncol_v, NEAR)
    place3, keep3, last3, here3 = columns(ncol - cluster * BLK, NEAR, lanes, subs)
    source = (ncol + padded(noff_v, NEAR) + LEAVES) & (LEAVES - 1)
    table[NB : NB + 1] = in_order(place3, index, lanes)
    table[NLEAF : NLEAF + 1] = in_order(place3, column(source, NEAR, lanes, subs), lanes)
    table[NKEEP : NKEEP + 1] = in_order(place3, keep3, lanes)
    table[NLAST : NLAST + 1] = last3
    table[NCOUNT : NCOUNT + 1] = here3


N_SEMS = 256
PLANE = [(a, b) for a in range(SIDE) for b in range(SIDE) if a or b]


def kernel(
    rhs_h, u_h, v_h, rank_h, row_h, col_h, near_h, ncol_h, noff_h,
    out_ref, hess_ref,
    rhs_v, u, v, near, rank_v, row_v, col_v, ncol_v, noff_v, table, idx,
    f0, f1, g0, g1, late0, late1, t, far_run, near_run, part0, part1, rs0, rs1,
    aa, ab, ba, bb, ca, cb,
    load_sem, send_sem, recv_sem,
):
    cluster, blk = lax.axis_index("cluster"), lax.axis_index("blk")
    y, z = cluster // SIDE, cluster % SIDE
    x, core = blk // 2, blk % 2
    count = [0]

    def new_ids(n):
        first = count[0]
        count[0] += n
        return range(first, first + n)

    def copy_of(i, src, dst, device):
        return pltpu.make_async_remote_copy(
            src_ref=src,
            dst_ref=dst,
            send_sem=send_sem.at[i],
            recv_sem=recv_sem.at[i],
            device_id=device,
            device_id_type=MESH,
        )

    def device(dy=0, dz=0, dx=0):
        there = ((y + dy) % SIDE) * SIDE + (z + dz) % SIDE
        return (there, ((x + dx) % SIDE) * 2 + core)

    def dev_blk(d):
        return (cluster, (blk + d) % BLK)

    mate = (cluster, blk + 1 - 2 * core)

    def in_plane(axis, a, b):
        return {"z": device(dy=a, dx=b), "y": device(dz=a, dx=b), "x": device(dy=a, dz=b)}[axis]

    def on_line(axis, d):
        return {"z": device(dz=d), "y": device(dy=d), "x": device(dx=d)}[axis]

    def per_core(action):
        for c in (0, 1):
            pl.when(core == c)(lambda c=c: action(c))

    barrier = pltpu.get_barrier_semaphore()
    partners = [dev_blk(d) for d in range(1, BLK)]
    partners += [device(dy=a, dz=b) for a, b in PLANE]
    partners += [device(dy=a, dx=b) for a, b in PLANE if a and b]
    partners += [device(dz=a, dx=b) for a, b in PLANE if a and b]
    for partner in partners:
        pl.semaphore_signal(barrier, inc=1, device_id=partner, device_id_type=MESH)
    loads = [
        (rhs_h, rhs_v), (rank_h, rank_v), (row_h, row_v), (col_h, col_v),
        (ncol_h, ncol_v), (noff_h, noff_v), (u_h, u), (near_h, near), (v_h, v),
    ]
    loads = [pltpu.make_async_copy(src, dst, load_sem.at[i]) for i, (src, dst) in enumerate(loads)]
    for load in loads:
        load.start()
    for load in loads[:6]:
        load.wait()

    def blk_round(buf, ids):
        return [copy_of(i, buf.at[blk], buf.at[blk], dev_blk(d)) for i, d in zip(ids, range(1, BLK))]

    def plane_round(buf, ids):
        return [copy_of(i, buf.at[cluster], buf.at[cluster], device(dy=a, dz=b)) for i, (a, b) in zip(ids, PLANE)]

    def start(copies):
        for copy in copies:
            copy.start()

    def landed(copies):
        for copy in copies:
            copy.wait_recv()

    def left(copies):
        for copy in copies:
            copy.wait_send()

    def total_start(tile, buf):
        buf[blk] = tile
        copies = blk_round(buf, new_ids(BLK - 1))
        start(copies)
        return copies

    def total_middle(copies, buf, buf_b):
        landed(copies)
        total = buf[0]
        for i in range(1, BLK):
            total = total + buf[i]
        buf_b[cluster] = total
        more = plane_round(buf_b, new_ids(len(PLANE)))
        start(more)
        return copies + more

    def total_end(copies, buf_b):
        landed(copies[BLK - 1 :])
        total = buf_b[0]
        for i in range(1, CLUSTERS):
            total = total + buf_b[i]
        left(copies)
        return total / PANELS

    def spread(f, ids):
        def copies(c):
            made = []
            for n, axis in enumerate(AXES):
                lo, size = ROW_CUT[c][axis]
                mine = f.at[y, z, x, c, pl.ds(lo, size)]
                for k, (a, b) in enumerate(PLANE):
                    made.append(copy_of(ids[n * len(PLANE) + k], mine, mine, in_plane(axis, a, b)))
            return made

        return copies

    def plane_leaf(ref, axis, i, c, rows):
        a, b = i // SIDE, i % SIDE
        place = {"z": (a, z, b), "y": (y, a, b), "x": (a, b, x)}[axis]
        return ref.at[place[0], place[1], place[2], c, rows]

    def each_held(c, action):
        for axis in AXES:
            lo, size = ROW_CUT[c][axis]
            for r in range(lo, lo + size, 16):
                rows, rhs = pl.ds(r, 16), slice(r // 2, r // 2 + 8)

                def step(i, carry, axis=axis, rows=rows, rhs=rhs):
                    action(axis, i, rows, rhs)
                    return carry

                lax.fori_loop(0, CLUSTERS, step, 0, unroll=4)

    class Lines:
        def __init__(self, g, late):
            self.g, self.late_slabs, self.line, self.mate = g, late, new_ids(9), new_ids(12)

        def slab(self, axis, c, d):
            lo, size = ROW_CUT[c][axis]
            rows = pl.ds(lo, size)
            if d == 2 and axis != "x":
                return self.late_slabs.at[AXES.index(axis), :, :, c, rows]
            if axis == "z":
                return self.g.at[:, (z + SIDE - d) % SIDE, :, c, rows]
            if axis == "y":
                return self.g.at[(y + SIDE - d) % SIDE, :, :, c, rows]
            return self.g.at[:, :, (x + SIDE - d) % SIDE, c, rows]

        def along(self, axis, c, d):
            own = self.slab(axis, c, 0)
            there = self.slab(axis, c, 2) if d == 2 and axis != "x" else own
            return copy_of(self.line[AXES.index(axis) * 3 + d - 1], own, there, on_line(axis, d))

        def across(self, axis, c, d):
            src = self.slab(axis, c, d)
            return copy_of(self.mate[AXES.index(axis) * 4 + d], src, src, mate)

        def begin(self, c):
            for axis, d in (("x", 1), ("x", 3), ("z", 1), ("z", 3), ("y", 1), ("y", 3), ("x", 2), ("z", 2), ("y", 2)):
                self.along(axis, c, d).start()
            for axis in AXES:
                self.across(axis, c, 0).start()

        def early(self, c):
            for axis, d in (("x", 1), ("x", 3), ("z", 1), ("z", 3), ("y", 1), ("y", 3), ("x", 2)):
                self.along(axis, c, d).wait_recv()
                self.across(axis, c, d).start()
            for axis in AXES:
                for d in (0, 1, 3):
                    self.across(axis, 1 - c, d).wait_recv()
            self.across("x", 1 - c, 2).wait_recv()

        def late(self, c):
            for axis in ("z", "y"):
                self.along(axis, c, 2).wait_recv()
                self.across(axis, c, 2).start()

        def last(self, c):
            for axis in ("z", "y"):
                self.across(axis, 1 - c, 2).wait_recv()

        def settle(self):
            for c in (0, 1):
                for n, axis in enumerate(AXES[:2]):
                    lo, size = ROW_CUT[c][axis]
                    rows = pl.ds(lo, size)
                    value = self.late_slabs[n, :, :, c, rows]
                    if axis == "z":
                        self.g[:, (z + 2) % SIDE, :, c, rows] = value
                    else:
                        self.g[(y + 2) % SIDE, :, :, c, rows] = value

        def end(self, c):
            for axis in AXES:
                for d in range(1, SIDE):
                    self.along(axis, c, d).wait_send()
                for d in range(SIDE):
                    self.across(axis, c, d).wait_send()

    lane = lax.broadcasted_iota(I32, (ROWS, LEAF), 1)
    zero = jnp.zeros((ROWS, LEAF), F32)

    def leaf_of(g, leaf):
        return g[leaf >> 5, (leaf >> 3) & 3, (leaf >> 1) & 3, leaf & 1]

    def apply_all(g, late, part):
        lines = Lines(g, late)
        per_core(lines.begin)

        def row_step(j, carry):
            c = conj_apply(leaf_of(g, idx[FLEAF, j]), u[idx[FB, j]])
            t[j] = jnp.where(lane < idx[FRANK, j], c, 0.0).astype(BF16)
            return carry

        def near_step(j, total):
            term = conj_apply(leaf_of(g, idx[NLEAF, j]), near[idx[NB, j]])
            total = jnp.where(idx[NKEEP, j] > 0, total, 0.0) + term
            near_run[j] = total
            return total

        def col_step(j, total):
            term = plain_apply(t[idx[CPOS, j]], v[idx[CB, j]])
            total = jnp.where(idx[CKEEP, j] > 0, total, 0.0) + term
            far_run[j] = total
            return total

        per_core(lines.early)
        lax.fori_loop(0, FIRST, row_step, 0, unroll=12)
        per_core(lines.late)
        lax.fori_loop(0, NEAR, near_step, zero, unroll=8)
        lax.fori_loop(0, FIRST, col_step, zero, unroll=12)
        per_core(lines.last)
        lines.settle()
        lax.fori_loop(FIRST, FAR, row_step, 0, unroll=14)
        lax.fori_loop(FIRST, FAR, col_step, zero, unroll=14)
        for l in range(BLK):
            one = jnp.where(idx[CCOUNT, l] > 0, far_run[idx[CLAST, l]], 0.0)
            two = jnp.where(idx[CCOUNT, l + BLK] > 0, far_run[idx[CLAST, l + BLK]], 0.0)
            three = jnp.where(idx[NCOUNT, l] > 0, near_run[idx[NLAST, l]], 0.0)
            part[l] = one + two + three
        return lines

    def reduce_scatter(part, rs):
        copies = []
        for i, d in zip(new_ids(BLK - 1), range(1, BLK)):
            copies.append(copy_of(i, part.at[(blk + d) % BLK], rs.at[blk], dev_blk(d)))
        start(copies)
        total = part[blk]
        landed(copies)
        for d in range(1, BLK):
            total = total + rs[(blk - d + BLK) % BLK]
        left(copies)
        return total

    for k in range(RHS // 8):
        f0[y, z, x, core, pl.ds(16 * k, 8)] = rhs_v[pl.ds(8 * k, 8)]
        f0[y, z, x, core, pl.ds(16 * k + 8, 8)] = rhs_v[pl.ds(RHS + 8 * k, 8)]
    a = rhs_v[...]
    tile = pack([a[:RHS] * a[:RHS] + a[RHS:] * a[RHS:]])
    pl.semaphore_wait(barrier, len(partners))
    total = total_start(tile, aa)
    first = spread(f0, new_ids(3 * len(PLANE)))
    per_core(lambda c: start(first(c)))
    total = total_middle(total, aa, ab)
    build_table(table, rank_v, row_v, col_v, ncol_v, noff_v, cluster, y, z)
    to_scalar = pltpu.make_async_copy(table, idx, load_sem.at[len(loads)])
    to_scalar.start()
    total = total_end(total, ab)
    scale = 1.0 / jnp.sqrt(unpack(total, 1)[0] + EPS)

    def first_q(c):
        landed(first(c))
        left(first(c))

        def action(axis, i, rows, rhs):
            held = plane_leaf(f0, axis, i, c, rows)
            q = held[...]
            q = join(re(q) * scale[rhs], im(q) * scale[rhs])
            held[...] = q
            plane_leaf(g0, axis, i, c, rows)[...] = q.astype(BF16)

        each_held(c, action)

    per_core(first_q)

    for load in loads[6:]:
        load.wait()
    to_scalar.wait()
    lines = apply_all(g0, late0, part0)
    w = reduce_scatter(part0, rs0)
    f1[y, z, x, core] = w
    q0 = f0[y, z, x, core]
    ws = w * DOWN

    def inner(a, b):
        return (
            re(a) * re(b) + im(a) * im(b),
            re(a) * im(b) - im(a) * re(b),
        )

    total = total_start(pack([*inner(q0, w), inner(ws, ws)[0], inner(q0, q0)[0]]), ba)
    second = spread(f1, new_ids(3 * len(PLANE)))
    per_core(lambda c: start(second(c)))
    total = total_middle(total, ba, bb)
    per_core(lines.end)
    total = total_end(total, bb)
    h00r, h00i, ww, g00 = unpack(total, 4)
    sr, si = h00r * DOWN, h00i * DOWN
    rr = ww - (sr * sr + si * si) * (2.0 - g00)
    h10 = jnp.sqrt(jnp.maximum(rr, 0.0) * UP * UP + EPS)
    scale1 = 1.0 / h10

    def second_q(c):
        landed(second(c))
        left(second(c))

        def action(axis, i, rows, rhs):
            held = plane_leaf(f1, axis, i, c, rows)
            w, q = held[...], plane_leaf(f0, axis, i, c, rows)[...]
            real = re(w) - (h00r[rhs] * re(q) - h00i[rhs] * im(q))
            imag = im(w) - (h00r[rhs] * im(q) + h00i[rhs] * re(q))
            q = join(real * scale1[rhs], imag * scale1[rhs])
            held[...] = q
            plane_leaf(g1, axis, i, c, rows)[...] = q.astype(BF16)

        each_held(c, action)

    per_core(second_q)

    lines = apply_all(g1, late1, part1)
    w = reduce_scatter(part1, rs1)
    q0, q1 = f0[y, z, x, core], f1[y, z, x, core]
    ws = w * DOWN
    tile = pack([*inner(q0, w), *inner(q1, w), inner(ws, ws)[0], inner(q1, q1)[0], *inner(q0, q1)])
    total = total_start(tile, ca)
    per_core(lines.end)
    total = total_end(total_middle(total, ca, cb), cb)
    ar, ai, br, bi, ww, g11, cr, ci = unpack(total, 8)
    real = re(w) - (ar * re(q0) - ai * im(q0)) - (br * re(q1) - bi * im(q1))
    imag = im(w) - (ar * im(q0) + ai * re(q0)) - (br * im(q1) + bi * re(q1))
    sar, sai, sbr, sbi = ar * DOWN, ai * DOWN, br * DOWN, bi * DOWN
    rr = ww - (sar * sar + sai * sai) * (2.0 - g00) - (sbr * sbr + sbi * sbi) * (2.0 - g11)
    pr, pi = sar * sbr + sai * sbi, sar * sbi - sai * sbr
    rr = rr + 2.0 * (pr * cr - pi * ci)
    h21 = jnp.sqrt(jnp.maximum(rr, 0.0) * UP * UP + EPS)
    out_ref[:RHS] = real / h21
    out_ref[RHS:] = imag / h21
    lanes = lane[:RHS]
    entries = jnp.zeros((RHS, LEAF), F32)
    for i, value in enumerate((h00r, h00i, h10, ar, ai, br, bi, h21)):
        entries = jnp.where(lanes == i, value, entries)
    hess_ref[...] = entries[:, :8]


def body(rhs, u, v, rank, row, col, near, ncol, noff):
    hbm = pl.BlockSpec(memory_space=pl.ANY)
    vmem = pl.BlockSpec(memory_space=pltpu.VMEM)
    grid = (SIDE, SIDE, SIDE, 2, ROWS, LEAF)
    late = pltpu.VMEM((2, SIDE, SIDE, 2, ROWS, LEAF), BF16)
    seg = pltpu.VMEM((BLK, ROWS, LEAF), F32)
    tiles8, tiles16 = pltpu.VMEM((BLK, 8, LEAF), F32), pltpu.VMEM((CLUSTERS, 8, LEAF), F32)
    out, hess = pl.pallas_call(
        kernel,
        out_shape=(
            jax.ShapeDtypeStruct((ROWS, LEAF), F32),
            jax.ShapeDtypeStruct((RHS, 8), F32),
        ),
        in_specs=[hbm] * 9,
        out_specs=(vmem, vmem),
        scratch_shapes=[
            pltpu.VMEM((ROWS, LEAF), F32),
            pltpu.VMEM((FAR, 2 * LEAF, LEAF), BF16),
            pltpu.VMEM((FAR, 2 * LEAF, LEAF), BF16),
            pltpu.VMEM((NEAR, 2 * LEAF, LEAF), BF16),
            pltpu.VMEM((FAR,), I32),
            pltpu.VMEM((FAR,), I32),
            pltpu.VMEM((FAR,), I32),
            pltpu.VMEM((NEAR,), I32),
            pltpu.VMEM((NEAR,), I32),
            pltpu.VMEM((16, LEAF), I32),
            pltpu.SMEM((16, LEAF), I32),
            pltpu.VMEM(grid, F32), pltpu.VMEM(grid, F32), pltpu.VMEM(grid, BF16), pltpu.VMEM(grid, BF16),
            late, late,
            pltpu.VMEM((FAR, ROWS, LEAF), BF16),
            pltpu.VMEM((FAR, ROWS, LEAF), F32),
            pltpu.VMEM((NEAR, ROWS, LEAF), F32),
            seg, seg, seg, seg,
            tiles8, tiles16, tiles8, tiles16, tiles8, tiles16,
            pltpu.SemaphoreType.DMA((16,)),
            pltpu.SemaphoreType.DMA((N_SEMS,)),
            pltpu.SemaphoreType.DMA((N_SEMS,)),
        ],
        compiler_params=pltpu.CompilerParams(
            collective_id=0, has_side_effects=True, vmem_limit_bytes=VMEM_BYTES
        ),
    )(
        rhs.reshape(ROWS, LEAF),
        u.reshape(FAR, 2 * LEAF, LEAF),
        v.reshape(FAR, 2 * LEAF, LEAF),
        rank, row, col,
        near.reshape(NEAR, 2 * LEAF, LEAF),
        ncol, noff,
    )
    return out.reshape(2, RHS, LEAF), hess


def solution(mesh):
    split = P(("cluster", "blk"))
    vector = P(None, None, ("cluster", "blk"))
    blocks = P(("cluster", "blk"), None, None, None)
    return jax.shard_map(
        body,
        mesh=mesh,
        in_specs=(vector, blocks, blocks, split, split, split, blocks, split, split),
        out_specs=(vector, P()),
        check_vma=False,
    )
```

time: 97.3 us -> 79.4 us (0.82)
  Pallas kernels: 88.8 us -> 75.8 us
  local copies, waits for them, and re-layouts: 6.89 us -> 2.75 us
    pallas_call x1, Pallas kernels: 88.8 us -> 75.8 us  [body(): pl.pallas_call(kernel, out_shape=(jax.ShapeDtypeStruct((ROWS, LEAF), F32)...]
    unnamed x16 -> x2, local copies, waits for them, and re-layouts: 6.89 us -> 2.75 us
where the time goes in v2:
time: 79.4 us; the launch traced here: 79.2 us
  Pallas kernels  75.8 us (95%)
  local copies, waits for them, and re-layouts  2.75 us (3%)
    pallas_call x1, Pallas kernels, body(): pl.pallas_call(kernel, out_shape=(jax.ShapeDtypeStruct((ROWS, LEAF), F32)...  75.8 us
    unnamed x2, local copies, waits for them, and re-layouts  2.75 us

profile of v2, /device:TPU:1, one launch (start us, length us, event | category | flops | bytes accessed | tf_op | source)
XLA Modules:
  0.0 79.2 jit_solution(13386050413994922899)
XLA Ops:
  0.6 75.8 %shard_map.104 = (f32[64,128]{1,0:T(8,128)}, f32[32,8]{1,0:T(8,128)}) custom-call(f32[64,128]{1,0:T(8,128)} %bitcast.8, bf16[64,256,128]{2,1,0:T(8,128)(2,1)} %bitcast.5, bf16[64,256,128]{2,1,0:T(8,128)(2,1)} %bitcast.6, s32[64]{0:T(128)} %rank_h.1, s32[64]{0:T(128)} %row_h.1, s32[64]{0:T(128)} %col_h.1, bf16[32,256,128]{2,1,0:T(8,128)(2,1)} %bitcast.7, ...), custom_call_target="tpu_custom_call" | custom-call | tf_op jit(solution)/shard_map/pallas_call | solution.py:522
  76.4 1.4 %copy.11 = f32[32,8]{0,1:T(8,128)} copy(f32[32,8]{1,0:T(8,128)} %get-tuple-element.7) | data formatting | bytes 2048
  77.8 1.4 %copy.13 = f32[2,32,128]{2,1,0:T(8,128)} copy(f32[2,32,128]{2,1,0:T(8,128)} %bitcast.9) | data formatting | bytes 65536

commit v3 on v2

--- a/solution.py
+++ b/solution.py
@@ -34,10 +34,6 @@
     return lax.dot_general(a, b, (((1,), (0,)), ((), ())), preferred_element_type=F32)
 
 
-def dot_nk(a, b):
-    return lax.dot_general(a, b, (((1,), (1,)), ((), ())), preferred_element_type=F32)
-
-
 def re(a):
     a = a.reshape(a.shape[0] // 16, 2, 8, LEAF)
     return a[:, 0].reshape(-1, LEAF)
@@ -60,9 +56,9 @@
 
 
 def plain_apply(t, w):
-    both = dot_nk(t, w)
-    real, imag = both[:, :LEAF], both[:, LEAF:]
-    return join(re(real) - im(imag), im(real) + re(imag))
+    wide = t.astype(F32)
+    turned = join(-im(wide), re(wide)).astype(BF16)
+    return dot_kn(jnp.concatenate([t, turned], axis=1), w)
 
 
 def pack(values):
@@ -160,7 +156,7 @@
     rhs_h, u_h, v_h, rank_h, row_h, col_h, near_h, ncol_h, noff_h,
     out_ref, hess_ref,
     rhs_v, u, v, near, rank_v, row_v, col_v, ncol_v, noff_v, table, idx,
-    f0, f1, g0, g1, late0, late1, t, far_run, near_run, part0, part1, rs0, rs1,
+    f0, f1, g0, g1, late0, late1, t, far_run, near_run, part0, part1, rs0, rs1, part0b, part1b, rs0b, rs1b,
     aa, ab, ba, bb, ca, cb,
     load_sem, send_sem, recv_sem,
 ):
@@ -212,7 +208,7 @@
         pl.semaphore_signal(barrier, inc=1, device_id=partner, device_id_type=MESH)
     loads = [
         (rhs_h, rhs_v), (rank_h, rank_v), (row_h, row_v), (col_h, col_v),
-        (ncol_h, ncol_v), (noff_h, noff_v), (u_h, u), (near_h, near), (v_h, v),
+        (ncol_h, ncol_v), (noff_h, noff_v), (v_h, v), (u_h, u), (near_h, near),
     ]
     loads = [pltpu.make_async_copy(src, dst, load_sem.at[i]) for i, (src, dst) in enumerate(loads)]
     for load in loads:
@@ -363,8 +359,8 @@
     def leaf_of(g, leaf):
         return g[leaf >> 5, (leaf >> 3) & 3, (leaf >> 1) & 3, leaf & 1]
 
-    def apply_all(g, late, part):
-        lines = Lines(g, late)
+    def apply_all(g, slabs, part, rs, part_b, rs_b):
+        lines = Lines(g, slabs)
         per_core(lines.begin)
 
         def row_step(j, carry):
@@ -385,32 +381,40 @@
             return total
 
         per_core(lines.early)
-        lax.fori_loop(0, FIRST, row_step, 0, unroll=12)
+        lax.fori_loop(0, FIRST, row_step, 0, unroll=FIRST)
         per_core(lines.late)
-        lax.fori_loop(0, NEAR, near_step, zero, unroll=8)
-        lax.fori_loop(0, FIRST, col_step, zero, unroll=12)
+        lax.fori_loop(0, NEAR, near_step, zero, unroll=NEAR)
+        lax.fori_loop(0, FIRST, col_step, zero, unroll=FIRST)
+        for l in range(BLK):
+            one = jnp.where(idx[CCOUNT, l] > 0, far_run[idx[CLAST, l]], 0.0)
+            two = jnp.where(idx[NCOUNT, l] > 0, near_run[idx[NLAST, l]], 0.0)
+            part[l] = one + two
+        early = scatter(part, rs)
+        start(early)
         per_core(lines.last)
         lines.settle()
-        lax.fori_loop(FIRST, FAR, row_step, 0, unroll=14)
-        lax.fori_loop(FIRST, FAR, col_step, zero, unroll=14)
+        lax.fori_loop(FIRST, FAR, row_step, 0, unroll=FAR - FIRST)
+        lax.fori_loop(FIRST, FAR, col_step, zero, unroll=FAR - FIRST)
         for l in range(BLK):
-            one = jnp.where(idx[CCOUNT, l] > 0, far_run[idx[CLAST, l]], 0.0)
-            two = jnp.where(idx[CCOUNT, l + BLK] > 0, far_run[idx[CLAST, l + BLK]], 0.0)
-            three = jnp.where(idx[NCOUNT, l] > 0, near_run[idx[NLAST, l]], 0.0)
-            part[l] = one + two + three
-        return lines
-
-    def reduce_scatter(part, rs):
+            part_b[l] = jnp.where(idx[CCOUNT, l + BLK] > 0, far_run[idx[CLAST, l + BLK]], 0.0).astype(BF16)
+        late = scatter(part_b, rs_b)
+        start(late)
+        mine = blk + BLK
+        total = part[blk] + jnp.where(idx[CCOUNT, mine] > 0, far_run[idx[CLAST, mine]], 0.0)
+        landed(early)
+        for d in range(1, BLK):
+            total = total + rs[(blk - d + BLK) % BLK]
+        landed(late)
+        for d in range(1, BLK):
+            total = total + rs_b[(blk - d + BLK) % BLK].astype(F32)
+        left(early + late)
+        return lines, total
+
+    def scatter(part, rs):
         copies = []
         for i, d in zip(new_ids(BLK - 1), range(1, BLK)):
             copies.append(copy_of(i, part.at[(blk + d) % BLK], rs.at[blk], dev_blk(d)))
-        start(copies)
-        total = part[blk]
-        landed(copies)
-        for d in range(1, BLK):
-            total = total + rs[(blk - d + BLK) % BLK]
-        left(copies)
-        return total
+        return copies
 
     for k in range(RHS // 8):
         f0[y, z, x, core, pl.ds(16 * k, 8)] = rhs_v[pl.ds(8 * k, 8)]
@@ -425,6 +429,14 @@
     build_table(table, rank_v, row_v, col_v, ncol_v, noff_v, cluster, y, z)
     to_scalar = pltpu.make_async_copy(table, idx, load_sem.at[len(loads)])
     to_scalar.start()
+    loads[6].wait()
+
+    def turn(k, carry):
+        w = v[k]
+        v[k] = jnp.concatenate([w[:LEAF].T, w[LEAF:].T], axis=0)
+        return carry
+
+    lax.fori_loop(0, FAR, turn, 0, unroll=8)
     total = total_end(total, ab)
     scale = 1.0 / jnp.sqrt(unpack(total, 1)[0] + EPS)
 
@@ -443,11 +455,10 @@
 
     per_core(first_q)
 
-    for load in loads[6:]:
+    for load in loads[7:]:
         load.wait()
     to_scalar.wait()
-    lines = apply_all(g0, late0, part0)
-    w = reduce_scatter(part0, rs0)
+    lines, w = apply_all(g0, late0, part0, rs0, part0b, rs0b)
     f1[y, z, x, core] = w
     q0 = f0[y, z, x, core]
     ws = w * DOWN
@@ -487,8 +498,7 @@
 
     per_core(second_q)
 
-    lines = apply_all(g1, late1, part1)
-    w = reduce_scatter(part1, rs1)
+    lines, w = apply_all(g1, late1, part1, rs1, part1b, rs1b)
     q0, q1 = f0[y, z, x, core], f1[y, z, x, core]
     ws = w * DOWN
     tile = pack([*inner(q0, w), *inner(q1, w), inner(ws, ws)[0], inner(q1, q1)[0], *inner(q0, q1)])
@@ -509,7 +519,19 @@
     entries = jnp.zeros((RHS, LEAF), F32)
     for i, value in enumerate((h00r, h00i, h10, ar, ai, br, bi, h21)):
         entries = jnp.where(lanes == i, value, entries)
-    hess_ref[...] = entries[:, :8]
+    entries = jnp.concatenate([entries, jnp.zeros((LEAF - RHS, LEAF), F32)], axis=0)
+    hess_ref[...] = entries.T[:8, :RHS]
+
+
+def publish(q_ref, h_ref, out_ref, hess_ref, sem):
+    copies = [
+        pltpu.make_async_copy(q_ref, out_ref, sem.at[0]),
+        pltpu.make_async_copy(h_ref, hess_ref, sem.at[1]),
+    ]
+    for copy in copies:
+        copy.start()
+    for copy in copies:
+        copy.wait()
 
 
 def body(rhs, u, v, rank, row, col, near, ncol, noff):
@@ -517,13 +539,13 @@
     vmem = pl.BlockSpec(memory_space=pltpu.VMEM)
     grid = (SIDE, SIDE, SIDE, 2, ROWS, LEAF)
     late = pltpu.VMEM((2, SIDE, SIDE, 2, ROWS, LEAF), BF16)
-    seg = pltpu.VMEM((BLK, ROWS, LEAF), F32)
+    seg, seg_b = pltpu.VMEM((BLK, ROWS, LEAF), F32), pltpu.VMEM((BLK, ROWS, LEAF), BF16)
     tiles8, tiles16 = pltpu.VMEM((BLK, 8, LEAF), F32), pltpu.VMEM((CLUSTERS, 8, LEAF), F32)
     out, hess = pl.pallas_call(
         kernel,
         out_shape=(
             jax.ShapeDtypeStruct((ROWS, LEAF), F32),
-            jax.ShapeDtypeStruct((RHS, 8), F32),
+            jax.ShapeDtypeStruct((8, RHS), F32),
         ),
         in_specs=[hbm] * 9,
         out_specs=(vmem, vmem),
@@ -544,7 +566,7 @@
             pltpu.VMEM((FAR, ROWS, LEAF), BF16),
             pltpu.VMEM((FAR, ROWS, LEAF), F32),
             pltpu.VMEM((NEAR, ROWS, LEAF), F32),
-            seg, seg, seg, seg,
+            seg, seg, seg, seg, seg_b, seg_b, seg_b, seg_b,
             tiles8, tiles16, tiles8, tiles16, tiles8, tiles16,
             pltpu.SemaphoreType.DMA((16,)),
             pltpu.SemaphoreType.DMA((N_SEMS,)),
@@ -561,7 +583,15 @@
         near.reshape(NEAR, 2 * LEAF, LEAF),
         ncol, noff,
     )
-    return out.reshape(2, RHS, LEAF), hess
+    out, hess = pl.pallas_call(
+        publish,
+        out_shape=(out, hess),
+        in_specs=[hbm, hbm],
+        out_specs=(hbm, hbm),
+        scratch_shapes=[pltpu.SemaphoreType.DMA((2,))],
+        compiler_params=pltpu.CompilerParams(vmem_limit_bytes=VMEM_BYTES),
+    )(out, hess)
+    return out.reshape(2, RHS, LEAF), hess.T
 
 
 def solution(mesh):

time: 79.4 us -> 74.8 us (0.942)
  local copies, waits for them, and re-layouts: 2.75 us -> 0 us
  Pallas kernels: 75.8 us -> 74 us
    pallas_call x1, Pallas kernels: 75.8 us -> 71.8 us  [body(): pl.pallas_call(kernel, out_shape=(jax.ShapeDtypeStruct((ROWS, LEAF), F32)...]
    unnamed x2 -> x0, local copies, waits for them, and re-layouts: 2.75 us -> none
    pallas_call x0 -> x1, Pallas kernels: none -> 2.24 us  [body(): pl.pallas_call(publish, out_shape=(out, hess), in_specs=[hbm, hbm], out_s...]
where the time goes in v3:
time: 74.8 us; the launch traced here: 74.7 us
  Pallas kernels  74 us (99%)
    pallas_call x1, Pallas kernels, body(): pl.pallas_call(kernel, out_shape=(jax.ShapeDtypeStruct((ROWS, LEAF), F32)...  71.8 us
    pallas_call x1, Pallas kernels, body(): pl.pallas_call(publish, out_shape=(out, hess), in_specs=[hbm, hbm], out_s...  2.24 us

profile of v3, /device:TPU:1, one launch (start us, length us, event | category | flops | bytes accessed | tf_op | source)
XLA Modules:
  0.0 74.7 jit_solution(18131392496976603657)
XLA Ops:
  0.6 71.8 %shard_map.104 = (f32[64,128]{1,0:T(8,128)}, f32[8,32]{1,0:T(8,128)}) custom-call(f32[64,128]{1,0:T(8,128)} %bitcast.9, bf16[64,256,128]{2,1,0:T(8,128)(2,1)} %bitcast.6, bf16[64,256,128]{2,1,0:T(8,128)(2,1)} %bitcast.7, s32[64]{0:T(128)} %rank_h.1, s32[64]{0:T(128)} %row_h.1, s32[64]{0:T(128)} %col_h.1, bf16[32,256,128]{2,1,0:T(8,128)(2,1)} %bitcast.8, ...), custom_call_target="tpu_custom_call" | custom-call | tf_op jit(solution)/shard_map/pallas_call | solution.py:544
  72.4 2.2 %shard_map.105 = (f32[64,128]{1,0:T(8,128)}, f32[8,32]{1,0:T(8,128)}) custom-call(f32[64,128]{1,0:T(8,128)} %get-tuple-element.6.q_ref, f32[8,32]{1,0:T(8,128)} %get-tuple-element.7.h_ref), custom_call_target="tpu_custom_call" | custom-call | tf_op jit(solution)/shard_map/pallas_call | solution.py:586

commit v4 on v3

--- a/solution.py
+++ b/solution.py
@@ -275,8 +275,8 @@
         place = {"z": (a, z, b), "y": (y, a, b), "x": (a, b, x)}[axis]
         return ref.at[place[0], place[1], place[2], c, rows]
 
-    def each_held(c, action):
-        for axis in AXES:
+    def each_held(c, action, lines):
+        for axis in ("x", "z", "y"):
             lo, size = ROW_CUT[c][axis]
             for r in range(lo, lo + size, 16):
                 rows, rhs = pl.ds(r, 16), slice(r // 2, r // 2 + 8)
@@ -285,7 +285,9 @@
                     action(axis, i, rows, rhs)
                     return carry
 
-                lax.fori_loop(0, CLUSTERS, step, 0, unroll=4)
+                lax.fori_loop(0, CLUSTERS, step, 0, unroll=16)
+            lines.begin(axis, c)
+        lines.share(c)
 
     class Lines:
         def __init__(self, g, late):
@@ -311,9 +313,11 @@
             src = self.slab(axis, c, d)
             return copy_of(self.mate[AXES.index(axis) * 4 + d], src, src, mate)
 
-        def begin(self, c):
-            for axis, d in (("x", 1), ("x", 3), ("z", 1), ("z", 3), ("y", 1), ("y", 3), ("x", 2), ("z", 2), ("y", 2)):
+        def begin(self, axis, c):
+            for d in (1, 3, 2):
                 self.along(axis, c, d).start()
+
+        def share(self, c):
             for axis in AXES:
                 self.across(axis, c, 0).start()
 
@@ -359,9 +363,7 @@
     def leaf_of(g, leaf):
         return g[leaf >> 5, (leaf >> 3) & 3, (leaf >> 1) & 3, leaf & 1]
 
-    def apply_all(g, slabs, part, rs, part_b, rs_b):
-        lines = Lines(g, slabs)
-        per_core(lines.begin)
+    def apply_all(lines, g, part, rs, part_b, rs_b):
 
         def row_step(j, carry):
             c = conj_apply(leaf_of(g, idx[FLEAF, j]), u[idx[FB, j]])
@@ -381,26 +383,28 @@
             return total
 
         per_core(lines.early)
+        lax.fori_loop(0, NEAR, near_step, zero, unroll=NEAR)
+        for l in range(BLK):
+            part[l] = jnp.where(idx[NCOUNT, l] > 0, near_run[idx[NLAST, l]], 0.0)
+        early = scatter(part, rs)
+        start(early)
         lax.fori_loop(0, FIRST, row_step, 0, unroll=FIRST)
         per_core(lines.late)
-        lax.fori_loop(0, NEAR, near_step, zero, unroll=NEAR)
         lax.fori_loop(0, FIRST, col_step, zero, unroll=FIRST)
-        for l in range(BLK):
-            one = jnp.where(idx[CCOUNT, l] > 0, far_run[idx[CLAST, l]], 0.0)
-            two = jnp.where(idx[NCOUNT, l] > 0, near_run[idx[NLAST, l]], 0.0)
-            part[l] = one + two
-        early = scatter(part, rs)
-        start(early)
         per_core(lines.last)
         lines.settle()
         lax.fori_loop(FIRST, FAR, row_step, 0, unroll=FAR - FIRST)
         lax.fori_loop(FIRST, FAR, col_step, zero, unroll=FAR - FIRST)
+
+        def far_sum(l):
+            one = jnp.where(idx[CCOUNT, l] > 0, far_run[idx[CLAST, l]], 0.0)
+            return one + jnp.where(idx[CCOUNT, l + BLK] > 0, far_run[idx[CLAST, l + BLK]], 0.0)
+
         for l in range(BLK):
-            part_b[l] = jnp.where(idx[CCOUNT, l + BLK] > 0, far_run[idx[CLAST, l + BLK]], 0.0).astype(BF16)
+            part_b[l] = far_sum(l).astype(BF16)
         late = scatter(part_b, rs_b)
         start(late)
-        mine = blk + BLK
-        total = part[blk] + jnp.where(idx[CCOUNT, mine] > 0, far_run[idx[CLAST, mine]], 0.0)
+        total = part[blk] + far_sum(blk)
         landed(early)
         for d in range(1, BLK):
             total = total + rs[(blk - d + BLK) % BLK]
@@ -408,7 +412,7 @@
         for d in range(1, BLK):
             total = total + rs_b[(blk - d + BLK) % BLK].astype(F32)
         left(early + late)
-        return lines, total
+        return total
 
     def scatter(part, rs):
         copies = []
@@ -451,14 +455,15 @@
             held[...] = q
             plane_leaf(g0, axis, i, c, rows)[...] = q.astype(BF16)
 
-        each_held(c, action)
-
+        each_held(c, action, lines)
+
+    lines = Lines(g0, late0)
     per_core(first_q)
 
     for load in loads[7:]:
         load.wait()
     to_scalar.wait()
-    lines, w = apply_all(g0, late0, part0, rs0, part0b, rs0b)
+    w = apply_all(lines, g0, part0, rs0, part0b, rs0b)
     f1[y, z, x, core] = w
     q0 = f0[y, z, x, core]
     ws = w * DOWN
@@ -494,11 +499,12 @@
             held[...] = q
             plane_leaf(g1, axis, i, c, rows)[...] = q.astype(BF16)
 
-        each_held(c, action)
-
+        each_held(c, action, lines)
+
+    lines = Lines(g1, late1)
     per_core(second_q)
 
-    lines, w = apply_all(g1, late1, part1, rs1, part1b, rs1b)
+    w = apply_all(lines, g1, part1, rs1, part1b, rs1b)
     q0, q1 = f0[y, z, x, core], f1[y, z, x, core]
     ws = w * DOWN
     tile = pack([*inner(q0, w), *inner(q1, w), inner(ws, ws)[0], inner(q1, q1)[0], *inner(q0, q1)])

time: 74.8 us -> 72.4 us (0.968)
  Pallas kernels: 74 us -> 71.7 us
    pallas_call x1, Pallas kernels: 71.8 us -> 69.4 us  [body(): pl.pallas_call(kernel, out_shape=(jax.ShapeDtypeStruct((ROWS, LEAF), F32)...]
where the time goes in v4:
time: 72.4 us; the launch traced here: 72.3 us
  Pallas kernels  71.7 us (99%)
    pallas_call x1, Pallas kernels, body(): pl.pallas_call(kernel, out_shape=(jax.ShapeDtypeStruct((ROWS, LEAF), F32)...  69.4 us
    pallas_call x1, Pallas kernels, body(): pl.pallas_call(publish, out_shape=(out, hess), in_specs=[hbm, hbm], out_s...  2.24 us

profile of v4, /device:TPU:1, one launch (start us, length us, event | category | flops | bytes accessed | tf_op | source)
XLA Modules:
  0.0 72.3 jit_solution(3166225278147863195)
XLA Ops:
  0.6 69.4 %shard_map.104 = (f32[64,128]{1,0:T(8,128)}, f32[8,32]{1,0:T(8,128)}) custom-call(f32[64,128]{1,0:T(8,128)} %bitcast.9, bf16[64,256,128]{2,1,0:T(8,128)(2,1)} %bitcast.6, bf16[64,256,128]{2,1,0:T(8,128)(2,1)} %bitcast.7, s32[64]{0:T(128)} %rank_h.1, s32[64]{0:T(128)} %row_h.1, s32[64]{0:T(128)} %col_h.1, bf16[32,256,128]{2,1,0:T(8,128)(2,1)} %bitcast.8, ...), custom_call_target="tpu_custom_call" | custom-call | tf_op jit(solution)/shard_map/pallas_call | solution.py:550
  70.1 2.2 %shard_map.105 = (f32[64,128]{1,0:T(8,128)}, f32[8,32]{1,0:T(8,128)}) custom-call(f32[64,128]{1,0:T(8,128)} %get-tuple-element.6.q_ref, f32[8,32]{1,0:T(8,128)} %get-tuple-element.7.h_ref), custom_call_target="tpu_custom_call" | custom-call | tf_op jit(solution)/shard_map/pallas_call | solution.py:592

commit v5 on v4

--- a/solution.py
+++ b/solution.py
@@ -129,7 +129,7 @@
         here = jnp.sum(jnp.where(own == lanes, 1, 0), axis=0, keepdims=True).astype(I32)
         return place, keep, jnp.maximum(upto - 1, 0), here
 
-    local = late * BLK + padded(col_v, FAR) - cluster * BLK
+    local = padded(col_v, FAR) - cluster * BLK
     place2, keep2, last2, here2 = columns(local, FAR, lanes, subs)
     table[CB : CB + 1] = in_order(place2, index, lanes)
     table[CPOS : CPOS + 1] = in_order(place2, place1, lanes)
@@ -150,6 +150,7 @@
 
 N_SEMS = 256
 PLANE = [(a, b) for a in range(SIDE) for b in range(SIDE) if a or b]
+PLANE.sort(key=lambda p: -sum(min(q, SIDE - q) for q in p))
 
 
 def kernel(
@@ -325,15 +326,13 @@
             for axis, d in (("x", 1), ("x", 3), ("z", 1), ("z", 3), ("y", 1), ("y", 3), ("x", 2)):
                 self.along(axis, c, d).wait_recv()
                 self.across(axis, c, d).start()
+            for axis in ("z", "y"):
+                self.along(axis, c, 2).wait_recv()
+                self.across(axis, c, 2).start()
             for axis in AXES:
                 for d in (0, 1, 3):
                     self.across(axis, 1 - c, d).wait_recv()
             self.across("x", 1 - c, 2).wait_recv()
-
-        def late(self, c):
-            for axis in ("z", "y"):
-                self.along(axis, c, 2).wait_recv()
-                self.across(axis, c, 2).start()
 
         def last(self, c):
             for axis in ("z", "y"):
@@ -389,16 +388,13 @@
         early = scatter(part, rs)
         start(early)
         lax.fori_loop(0, FIRST, row_step, 0, unroll=FIRST)
-        per_core(lines.late)
-        lax.fori_loop(0, FIRST, col_step, zero, unroll=FIRST)
         per_core(lines.last)
         lines.settle()
         lax.fori_loop(FIRST, FAR, row_step, 0, unroll=FAR - FIRST)
-        lax.fori_loop(FIRST, FAR, col_step, zero, unroll=FAR - FIRST)
+        lax.fori_loop(0, FAR, col_step, zero, unroll=FAR)
 
         def far_sum(l):
-            one = jnp.where(idx[CCOUNT, l] > 0, far_run[idx[CLAST, l]], 0.0)
-            return one + jnp.where(idx[CCOUNT, l + BLK] > 0, far_run[idx[CLAST, l + BLK]], 0.0)
+            return jnp.where(idx[CCOUNT, l] > 0, far_run[idx[CLAST, l]], 0.0)
 
         for l in range(BLK):
             part_b[l] = far_sum(l).astype(BF16)

time: 72.4 us -> 70.5 us (0.974)
  Pallas kernels: 71.7 us -> 69.7 us
    pallas_call x1, Pallas kernels: 69.4 us -> 67.5 us  [body(): pl.pallas_call(kernel, out_shape=(jax.ShapeDtypeStruct((ROWS, LEAF), F32)...]
where the time goes in v5:
time: 70.5 us; the launch traced here: 70.4 us
  Pallas kernels  69.7 us (99%)
    pallas_call x1, Pallas kernels, body(): pl.pallas_call(kernel, out_shape=(jax.ShapeDtypeStruct((ROWS, LEAF), F32)...  67.5 us
    pallas_call x1, Pallas kernels, body(): pl.pallas_call(publish, out_shape=(out, hess), in_specs=[hbm, hbm], out_s...  2.24 us

profile of v5, /device:TPU:1, one launch (start us, length us, event | category | flops | bytes accessed | tf_op | source)
XLA Modules:
  0.0 70.4 jit_solution(11876697588362245438)
XLA Ops:
  0.6 67.5 %shard_map.104 = (f32[64,128]{1,0:T(8,128)}, f32[8,32]{1,0:T(8,128)}) custom-call(f32[64,128]{1,0:T(8,128)} %bitcast.9, bf16[64,256,128]{2,1,0:T(8,128)(2,1)} %bitcast.6, bf16[64,256,128]{2,1,0:T(8,128)(2,1)} %bitcast.7, s32[64]{0:T(128)} %rank_h.1, s32[64]{0:T(128)} %row_h.1, s32[64]{0:T(128)} %col_h.1, bf16[32,256,128]{2,1,0:T(8,128)(2,1)} %bitcast.8, ...), custom_call_target="tpu_custom_call" | custom-call | tf_op jit(solution)/shard_map/pallas_call | solution.py:546
  68.1 2.2 %shard_map.105 = (f32[64,128]{1,0:T(8,128)}, f32[8,32]{1,0:T(8,128)}) custom-call(f32[64,128]{1,0:T(8,128)} %get-tuple-element.6.q_ref, f32[8,32]{1,0:T(8,128)} %get-tuple-element.7.h_ref), custom_call_target="tpu_custom_call" | custom-call | tf_op jit(solution)/shard_map/pallas_call | solution.py:588

commit v6 on v5

--- a/solution.py
+++ b/solution.py
@@ -157,7 +157,7 @@
     rhs_h, u_h, v_h, rank_h, row_h, col_h, near_h, ncol_h, noff_h,
     out_ref, hess_ref,
     rhs_v, u, v, near, rank_v, row_v, col_v, ncol_v, noff_v, table, idx,
-    f0, f1, g0, g1, late0, late1, t, far_run, near_run, part0, part1, rs0, rs1, part0b, part1b, rs0b, rs1b,
+    f0, f1, g0, g1, late0, late1, t, far_run, near_run, rest, part0a, part1a, rs0a, rs1a, part0b, part1b, rs0b, rs1b,
     aa, ab, ba, bb, ca, cb,
     load_sem, send_sem, recv_sem,
 ):
@@ -277,7 +277,7 @@
         return ref.at[place[0], place[1], place[2], c, rows]
 
     def each_held(c, action, lines):
-        for axis in ("x", "z", "y"):
+        for axis in AXES:
             lo, size = ROW_CUT[c][axis]
             for r in range(lo, lo + size, 16):
                 rows, rhs = pl.ds(r, 16), slice(r // 2, r // 2 + 8)
@@ -362,7 +362,7 @@
     def leaf_of(g, leaf):
         return g[leaf >> 5, (leaf >> 3) & 3, (leaf >> 1) & 3, leaf & 1]
 
-    def apply_all(lines, g, part, rs, part_b, rs_b):
+    def apply_all(lines, g, part_a, rs_a, part_b, rs_b):
 
         def row_step(j, carry):
             c = conj_apply(leaf_of(g, idx[FLEAF, j]), u[idx[FB, j]])
@@ -384,8 +384,11 @@
         per_core(lines.early)
         lax.fori_loop(0, NEAR, near_step, zero, unroll=NEAR)
         for l in range(BLK):
-            part[l] = jnp.where(idx[NCOUNT, l] > 0, near_run[idx[NLAST, l]], 0.0)
-        early = scatter(part, rs)
+            near_sum = jnp.where(idx[NCOUNT, l] > 0, near_run[idx[NLAST, l]], 0.0)
+            rounded = near_sum.astype(BF16)
+            part_a[l] = rounded
+            rest[l] = near_sum - rounded.astype(F32)
+        early = scatter(part_a, rs_a)
         start(early)
         lax.fori_loop(0, FIRST, row_step, 0, unroll=FIRST)
         per_core(lines.last)
@@ -397,13 +400,13 @@
             return jnp.where(idx[CCOUNT, l] > 0, far_run[idx[CLAST, l]], 0.0)
 
         for l in range(BLK):
-            part_b[l] = far_sum(l).astype(BF16)
+            part_b[l] = (far_sum(l) + rest[l]).astype(BF16)
         late = scatter(part_b, rs_b)
         start(late)
-        total = part[blk] + far_sum(blk)
+        total = part_a[blk].astype(F32) + rest[blk] + far_sum(blk)
         landed(early)
         for d in range(1, BLK):
-            total = total + rs[(blk - d + BLK) % BLK]
+            total = total + rs_a[(blk - d + BLK) % BLK].astype(F32)
         landed(late)
         for d in range(1, BLK):
             total = total + rs_b[(blk - d + BLK) % BLK].astype(F32)
@@ -459,7 +462,7 @@
     for load in loads[7:]:
         load.wait()
     to_scalar.wait()
-    w = apply_all(lines, g0, part0, rs0, part0b, rs0b)
+    w = apply_all(lines, g0, part0a, rs0a, part0b, rs0b)
     f1[y, z, x, core] = w
     q0 = f0[y, z, x, core]
     ws = w * DOWN
@@ -500,7 +503,7 @@
     lines = Lines(g1, late1)
     per_core(second_q)
 
-    w = apply_all(lines, g1, part1, rs1, part1b, rs1b)
+    w = apply_all(lines, g1, part1a, rs1a, part1b, rs1b)
     q0, q1 = f0[y, z, x, core], f1[y, z, x, core]
     ws = w * DOWN
     tile = pack([*inner(q0, w), *inner(q1, w), inner(ws, ws)[0], inner(q1, q1)[0], *inner(q0, q1)])
@@ -568,7 +571,7 @@
             pltpu.VMEM((FAR, ROWS, LEAF), BF16),
             pltpu.VMEM((FAR, ROWS, LEAF), F32),
             pltpu.VMEM((NEAR, ROWS, LEAF), F32),
-            seg, seg, seg, seg, seg_b, seg_b, seg_b, seg_b,
+            seg, seg_b, seg_b, seg_b, seg_b, seg_b, seg_b, seg_b, seg_b,
             tiles8, tiles16, tiles8, tiles16, tiles8, tiles16,
             pltpu.SemaphoreType.DMA((16,)),
             pltpu.SemaphoreType.DMA((N_SEMS,)),

time: 70.5 us -> 69.1 us (0.980)
  Pallas kernels: 69.7 us -> 68.4 us
    pallas_call x1, Pallas kernels: 67.5 us -> 66.1 us  [body(): pl.pallas_call(kernel, out_shape=(jax.ShapeDtypeStruct((ROWS, LEAF), F32)...]
where the time goes in v6:
time: 69.1 us; the launch traced here: 69 us
  Pallas kernels  68.4 us (99%)
    pallas_call x1, Pallas kernels, body(): pl.pallas_call(kernel, out_shape=(jax.ShapeDtypeStruct((ROWS, LEAF), F32)...  66.1 us
    pallas_call x1, Pallas kernels, body(): pl.pallas_call(publish, out_shape=(out, hess), in_specs=[hbm, hbm], out_s...  2.24 us

profile of v6, /device:TPU:1, one launch (start us, length us, event | category | flops | bytes accessed | tf_op | source)
XLA Modules:
  0.0 69.0 jit_solution(14979080014665107327)
XLA Ops:
  0.6 66.1 %shard_map.104 = (f32[64,128]{1,0:T(8,128)}, f32[8,32]{1,0:T(8,128)}) custom-call(f32[64,128]{1,0:T(8,128)} %bitcast.9, bf16[64,256,128]{2,1,0:T(8,128)(2,1)} %bitcast.6, bf16[64,256,128]{2,1,0:T(8,128)(2,1)} %bitcast.7, s32[64]{0:T(128)} %rank_h.1, s32[64]{0:T(128)} %row_h.1, s32[64]{0:T(128)} %col_h.1, bf16[32,256,128]{2,1,0:T(8,128)(2,1)} %bitcast.8, ...), custom_call_target="tpu_custom_call" | custom-call | tf_op jit(solution)/shard_map/pallas_call | solution.py:549
  66.8 2.2 %shard_map.105 = (f32[64,128]{1,0:T(8,128)}, f32[8,32]{1,0:T(8,128)}) custom-call(f32[64,128]{1,0:T(8,128)} %get-tuple-element.6.q_ref, f32[8,32]{1,0:T(8,128)} %get-tuple-element.7.h_ref), custom_call_target="tpu_custom_call" | custom-call | tf_op jit(solution)/shard_map/pallas_call | solution.py:591

commit v7 on v6

--- a/solution.py
+++ b/solution.py
@@ -68,8 +68,7 @@
         four = values[i : i + 4]
         four = jnp.concatenate(four + [zero] * (4 - len(four)), axis=0)
         rows.append(jnp.sum(four.T, axis=0, keepdims=True))
-    rows.append(jnp.zeros((8 - len(rows), LEAF), F32))
-    return jnp.concatenate(rows, axis=0)
+    return jnp.concatenate(rows, axis=0) if len(rows) > 1 else rows[0]
 
 
 def unpack(tile, count):
@@ -149,6 +148,7 @@
 
 
 N_SEMS = 256
+AROUND = (4, 3, 5, 2, 6, 1, 7)
 PLANE = [(a, b) for a in range(SIDE) for b in range(SIDE) if a or b]
 PLANE.sort(key=lambda p: -sum(min(q, SIDE - q) for q in p))
 
@@ -218,7 +218,7 @@
         load.wait()
 
     def blk_round(buf, ids):
-        return [copy_of(i, buf.at[blk], buf.at[blk], dev_blk(d)) for i, d in zip(ids, range(1, BLK))]
+        return [copy_of(i, buf.at[blk], buf.at[blk], dev_blk(d)) for i, d in zip(ids, AROUND)]
 
     def plane_round(buf, ids):
         return [copy_of(i, buf.at[cluster], buf.at[cluster], device(dy=a, dz=b)) for i, (a, b) in zip(ids, PLANE)]
@@ -276,8 +276,11 @@
         place = {"z": (a, z, b), "y": (y, a, b), "x": (a, b, x)}[axis]
         return ref.at[place[0], place[1], place[2], c, rows]
 
-    def each_held(c, action, lines):
-        for axis in AXES:
+    def each_held(c, action, copies, lines):
+        for n, axis in enumerate(AXES):
+            group = copies[n * len(PLANE) : (n + 1) * len(PLANE)]
+            landed(group)
+            left(group)
             lo, size = ROW_CUT[c][axis]
             for r in range(lo, lo + size, 16):
                 rows, rhs = pl.ds(r, 16), slice(r // 2, r // 2 + 8)
@@ -415,7 +418,7 @@
 
     def scatter(part, rs):
         copies = []
-        for i, d in zip(new_ids(BLK - 1), range(1, BLK)):
+        for i, d in zip(new_ids(BLK - 1), AROUND):
             copies.append(copy_of(i, part.at[(blk + d) % BLK], rs.at[blk], dev_blk(d)))
         return copies
 
@@ -444,8 +447,6 @@
     scale = 1.0 / jnp.sqrt(unpack(total, 1)[0] + EPS)
 
     def first_q(c):
-        landed(first(c))
-        left(first(c))
 
         def action(axis, i, rows, rhs):
             held = plane_leaf(f0, axis, i, c, rows)
@@ -454,7 +455,7 @@
             held[...] = q
             plane_leaf(g0, axis, i, c, rows)[...] = q.astype(BF16)
 
-        each_held(c, action, lines)
+        each_held(c, action, first(c), lines)
 
     lines = Lines(g0, late0)
     per_core(first_q)
@@ -486,8 +487,6 @@
     scale1 = 1.0 / h10
 
     def second_q(c):
-        landed(second(c))
-        left(second(c))
 
         def action(axis, i, rows, rhs):
             held = plane_leaf(f1, axis, i, c, rows)
@@ -498,7 +497,7 @@
             held[...] = q
             plane_leaf(g1, axis, i, c, rows)[...] = q.astype(BF16)
 
-        each_held(c, action, lines)
+        each_held(c, action, second(c), lines)
 
     lines = Lines(g1, late1)
     per_core(second_q)
@@ -545,7 +544,7 @@
     grid = (SIDE, SIDE, SIDE, 2, ROWS, LEAF)
     late = pltpu.VMEM((2, SIDE, SIDE, 2, ROWS, LEAF), BF16)
     seg, seg_b = pltpu.VMEM((BLK, ROWS, LEAF), F32), pltpu.VMEM((BLK, ROWS, LEAF), BF16)
-    tiles8, tiles16 = pltpu.VMEM((BLK, 8, LEAF), F32), pltpu.VMEM((CLUSTERS, 8, LEAF), F32)
+    sums = [pltpu.VMEM((n, rows, LEAF), F32) for rows in (1, 1, 2) for n in (BLK, CLUSTERS)]
     out, hess = pl.pallas_call(
         kernel,
         out_shape=(
@@ -572,7 +571,7 @@
             pltpu.VMEM((FAR, ROWS, LEAF), F32),
             pltpu.VMEM((NEAR, ROWS, LEAF), F32),
             seg, seg_b, seg_b, seg_b, seg_b, seg_b, seg_b, seg_b, seg_b,
-            tiles8, tiles16, tiles8, tiles16, tiles8, tiles16,
+            *sums,
             pltpu.SemaphoreType.DMA((16,)),
             pltpu.SemaphoreType.DMA((N_SEMS,)),
             pltpu.SemaphoreType.DMA((N_SEMS,)),

time: 69.1 us -> 66.4 us (0.961)
  Pallas kernels: 68.4 us -> 65.7 us
    pallas_call x1, Pallas kernels: 66.1 us -> 63.5 us  [body(): pl.pallas_call(kernel, out_shape=(jax.ShapeDtypeStruct((ROWS, LEAF), F32)...]
where the time goes in v7:
time: 66.4 us; the launch traced here: 66.3 us
  Pallas kernels  65.7 us (99%)
    pallas_call x1, Pallas kernels, body(): pl.pallas_call(kernel, out_shape=(jax.ShapeDtypeStruct((ROWS, LEAF), F32)...  63.5 us
    pallas_call x1, Pallas kernels, body(): pl.pallas_call(publish, out_shape=(out, hess), in_specs=[hbm, hbm], out_s...  2.24 us

profile of v7, /device:TPU:1, one launch (start us, length us, event | category | flops | bytes accessed | tf_op | source)
XLA Modules:
  0.0 66.3 jit_solution(347264478070867502)
XLA Ops:
  0.6 63.5 %shard_map.104 = (f32[64,128]{1,0:T(8,128)}, f32[8,32]{1,0:T(8,128)}) custom-call(f32[64,128]{1,0:T(8,128)} %bitcast.9, bf16[64,256,128]{2,1,0:T(8,128)(2,1)} %bitcast.6, bf16[64,256,128]{2,1,0:T(8,128)(2,1)} %bitcast.7, s32[64]{0:T(128)} %rank_h.1, s32[64]{0:T(128)} %row_h.1, s32[64]{0:T(128)} %col_h.1, bf16[32,256,128]{2,1,0:T(8,128)(2,1)} %bitcast.8, ...), custom_call_target="tpu_custom_call" | custom-call | tf_op jit(solution)/shard_map/pallas_call | solution.py:548
  64.1 2.2 %shard_map.105 = (f32[64,128]{1,0:T(8,128)}, f32[8,32]{1,0:T(8,128)}) custom-call(f32[64,128]{1,0:T(8,128)} %get-tuple-element.6.q_ref, f32[8,32]{1,0:T(8,128)} %get-tuple-element.7.h_ref), custom_call_target="tpu_custom_call" | custom-call | tf_op jit(solution)/shard_map/pallas_call | solution.py:590

commit v8 on v7

--- a/solution.py
+++ b/solution.py
@@ -527,15 +527,9 @@
     hess_ref[...] = entries.T[:8, :RHS]
 
 
-def publish(q_ref, h_ref, out_ref, hess_ref, sem):
-    copies = [
-        pltpu.make_async_copy(q_ref, out_ref, sem.at[0]),
-        pltpu.make_async_copy(h_ref, hess_ref, sem.at[1]),
-    ]
-    for copy in copies:
-        copy.start()
-    for copy in copies:
-        copy.wait()
+def publish(q_ref, h_ref, out_ref, hess_ref):
+    out_ref[...] = q_ref[...]
+    hess_ref[...] = h_ref[...]
 
 
 def body(rhs, u, v, rank, row, col, near, ncol, noff):
@@ -590,9 +584,8 @@
     out, hess = pl.pallas_call(
         publish,
         out_shape=(out, hess),
-        in_specs=[hbm, hbm],
-        out_specs=(hbm, hbm),
-        scratch_shapes=[pltpu.SemaphoreType.DMA((2,))],
+        in_specs=[vmem, vmem],
+        out_specs=(vmem, vmem),
         compiler_params=pltpu.CompilerParams(vmem_limit_bytes=VMEM_BYTES),
     )(out, hess)
     return out.reshape(2, RHS, LEAF), hess.T

time: 66.4 us -> 65.7 us (0.989)
  Pallas kernels: 65.7 us -> 64.9 us
    pallas_call x1, Pallas kernels: 2.24 us -> 1.38 us  [body(): pl.pallas_call(publish, out_shape=(out, hess), in_specs=[vmem, vmem], out...]
where the time goes in v8:
time: 65.7 us; the launch traced here: 65.5 us
  Pallas kernels  64.9 us (99%)
    pallas_call x1, Pallas kernels, body(): pl.pallas_call(kernel, out_shape=(jax.ShapeDtypeStruct((ROWS, LEAF), F32)...  63.5 us
    pallas_call x1, Pallas kernels, body(): pl.pallas_call(publish, out_shape=(out, hess), in_specs=[vmem, vmem], out...  1.38 us

profile of v8, /device:TPU:1, one launch (start us, length us, event | category | flops | bytes accessed | tf_op | source)
XLA Modules:
  0.0 65.5 jit_solution(12446764511622166793)
XLA Ops:
  0.6 63.5 %shard_map.104 = (f32[64,128]{1,0:T(8,128)}, f32[8,32]{1,0:T(8,128)}) custom-call(f32[64,128]{1,0:T(8,128)} %bitcast.9, bf16[64,256,128]{2,1,0:T(8,128)(2,1)} %bitcast.6, bf16[64,256,128]{2,1,0:T(8,128)(2,1)} %bitcast.7, s32[64]{0:T(128)} %rank_h.1, s32[64]{0:T(128)} %row_h.1, s32[64]{0:T(128)} %col_h.1, bf16[32,256,128]{2,1,0:T(8,128)(2,1)} %bitcast.8, ...), custom_call_target="tpu_custom_call" | custom-call | tf_op jit(solution)/shard_map/pallas_call | solution.py:542
  64.2 1.4 %shard_map.105 = (f32[64,128]{1,0:T(8,128)}, f32[8,32]{1,0:T(8,128)}) custom-call(f32[64,128]{1,0:T(8,128)} %get-tuple-element.6.q_ref, f32[8,32]{1,0:T(8,128)} %get-tuple-element.7.h_ref), custom_call_target="tpu_custom_call" | custom-call | tf_op jit(solution)/shard_map/pallas_call | solution.py:584

commit v9 on v8

--- a/solution.py
+++ b/solution.py
@@ -128,7 +128,7 @@
         here = jnp.sum(jnp.where(own == lanes, 1, 0), axis=0, keepdims=True).astype(I32)
         return place, keep, jnp.maximum(upto - 1, 0), here
 
-    local = padded(col_v, FAR) - cluster * BLK
+    local = late * BLK + padded(col_v, FAR) - cluster * BLK
     place2, keep2, last2, here2 = columns(local, FAR, lanes, subs)
     table[CB : CB + 1] = in_order(place2, index, lanes)
     table[CPOS : CPOS + 1] = in_order(place2, place1, lanes)
@@ -394,13 +394,15 @@
         early = scatter(part_a, rs_a)
         start(early)
         lax.fori_loop(0, FIRST, row_step, 0, unroll=FIRST)
+        lax.fori_loop(0, FIRST, col_step, zero, unroll=FIRST)
         per_core(lines.last)
         lines.settle()
         lax.fori_loop(FIRST, FAR, row_step, 0, unroll=FAR - FIRST)
-        lax.fori_loop(0, FAR, col_step, zero, unroll=FAR)
+        lax.fori_loop(FIRST, FAR, col_step, zero, unroll=FAR - FIRST)
 
         def far_sum(l):
-            return jnp.where(idx[CCOUNT, l] > 0, far_run[idx[CLAST, l]], 0.0)
+            one = jnp.where(idx[CCOUNT, l] > 0, far_run[idx[CLAST, l]], 0.0)
+            return one + jnp.where(idx[CCOUNT, l + BLK] > 0, far_run[idx[CLAST, l + BLK]], 0.0)
 
         for l in range(BLK):
             part_b[l] = (far_sum(l) + rest[l]).astype(BF16)

time: 65.7 us -> 65.8 us (level)
  no operation moved by 1% of the time
where the time goes in v9:
time: 65.8 us; the launch traced here: 65.7 us
  Pallas kernels  65 us (99%)
    pallas_call x1, Pallas kernels, body(): pl.pallas_call(kernel, out_shape=(jax.ShapeDtypeStruct((ROWS, LEAF), F32)...  63.6 us
    pallas_call x1, Pallas kernels, body(): pl.pallas_call(publish, out_shape=(out, hess), in_specs=[vmem, vmem], out...  1.38 us

profile of v9, /device:TPU:1, one launch (start us, length us, event | category | flops | bytes accessed | tf_op | source)
XLA Modules:
  0.0 65.7 jit_solution(17385499055404902882)
XLA Ops:
  0.6 63.6 %shard_map.104 = (f32[64,128]{1,0:T(8,128)}, f32[8,32]{1,0:T(8,128)}) custom-call(f32[64,128]{1,0:T(8,128)} %bitcast.9, bf16[64,256,128]{2,1,0:T(8,128)(2,1)} %bitcast.6, bf16[64,256,128]{2,1,0:T(8,128)(2,1)} %bitcast.7, s32[64]{0:T(128)} %rank_h.1, s32[64]{0:T(128)} %row_h.1, s32[64]{0:T(128)} %col_h.1, bf16[32,256,128]{2,1,0:T(8,128)(2,1)} %bitcast.8, ...), custom_call_target="tpu_custom_call" | custom-call | tf_op jit(solution)/shard_map/pallas_call | solution.py:544
  64.3 1.4 %shard_map.105 = (f32[64,128]{1,0:T(8,128)}, f32[8,32]{1,0:T(8,128)}) custom-call(f32[64,128]{1,0:T(8,128)} %get-tuple-element.6.q_ref, f32[8,32]{1,0:T(8,128)} %get-tuple-element.7.h_ref), custom_call_target="tpu_custom_call" | custom-call | tf_op jit(solution)/shard_map/pallas_call | solution.py:586
